TPU v7x, 32 devices: a whole 2x2x4 slice. The times are simulated.
32 devices in a mesh: ga: 2 (over y), gx: 2 (over core), yz: 8 (over z, x).
Axes of the slice: x: 2, y: 2, z: 4, core: 2. Of those that a mesh axis runs over, the one named last changes fastest.
Arguments:
- tokens: bfloat16 [32, 18432], P(('ga', 'yz'), 'gx'), parts along dimension 0, may hold values from -6 to 6
- gain: float32 [18432], P('gx'), may hold values from 0.5 to 1.5
- w_qkv: bfloat16 [18432, 12800], P('gx', 'yz'), may hold values from -0.046875 to 0.046875
- kv_cache: bfloat16 [32, 512, 512], P(('ga', 'yz', 'gx')), parts along dimension 0, may hold values from -256 to 256
- lengths: int32 [32], P(('ga', 'yz', 'gx')), parts along dimension 0, may hold values from 2 to 512, as said below
- w_out: bfloat16 [12288, 18432], P('gx', 'yz'), may hold values from -0.0546875 to 0.0546875
Outputs:
- attn_out: bfloat16 [32, 18432], P(('ga', 'gx'), 'yz'), parts along dimension 0
There are 2 independent parts, one for each index of `ga`. A program takes and returns all parts, laid end to end along the dimension named above; an argument that names none is the same for every part. Nothing has to cross between parts.
Inputs may be any that keep to these rules, and one draw needn't show every extreme that they name: `lengths`: every sequence holds at least 2 cached positions; some sequence holds exactly 512.
All inputs are finite; a program needn't handle non-finite values.
Results may differ from a plain program's by a relative error of at most 0.012.
The roundings to bfloat16 on the way count: a program that leaves them out, or rounds other values in their place, can miss the bound.
Values may be sent and summed in bfloat16 or wider, within the bound.
No kernel may reach another device: no remote copies, remote signals or barrier semaphores. Data moves between devices by JAX's collectives and lax.ppermute only.
A program may use at most 128 MiB of HBM per device.

v0:
```python
import jax
import jax.numpy as jnp
from jax import lax
from jax.sharding import PartitionSpec as P

D = 18432
HQ = 48
HD = 256


def scale_rows(values, sums, gain):
    mean = sums[0] / D
    var = sums[1] / D - mean * mean
    centered = values.astype(jnp.float32) - mean[:, None]
    return (centered * lax.rsqrt(var + 1e-06)[:, None] * gain[None, :]).astype(jnp.bfloat16)


def row_sums(values):
    values_f = values.astype(jnp.float32)
    return (jnp.sum(values_f, axis=1), jnp.sum(values_f * values_f, axis=1))


def attend(qkv, kv_cache, lengths):
    seqs = qkv.shape[0]
    query = qkv[:, : HQ * HD].reshape(seqs, HQ, HD)
    key_new = qkv[:, HQ * HD : HQ * HD + HD]
    value_new = qkv[:, HQ * HD + HD :]
    keys = kv_cache[:, :, :HD]
    values = kv_cache[:, :, HD:]
    scores = jnp.einsum("bhd,bsd->bhs", query, keys, preferred_element_type=jnp.float32) / 16.0
    score_new = jnp.einsum("bhd,bd->bh", query, key_new, preferred_element_type=jnp.float32) / 16.0
    valid = jnp.arange(kv_cache.shape[1], dtype=jnp.int32)[None, None, :] < lengths[:, None, None]
    masked = jnp.where(valid, scores, -1e30)
    top = jnp.maximum(jnp.max(masked, axis=2), score_new)
    expd = jnp.where(valid, jnp.exp(masked - top[:, :, None]), 0.0)
    exp_new = jnp.exp(score_new - top)
    total = jnp.sum(expd, axis=2) + exp_new
    probs = (expd / total[:, :, None]).astype(jnp.bfloat16)
    prob_new = (exp_new / total).astype(jnp.bfloat16)
    attended = jnp.einsum("bhs,bsd->bhd", probs, values, preferred_element_type=jnp.float32)
    attended = (
        attended
        + prob_new.astype(jnp.float32)[:, :, None] * value_new.astype(jnp.float32)[:, None, :]
    )
    return attended.astype(jnp.bfloat16).reshape(seqs, HQ * HD)


def on_device(tokens, gain, w_qkv, kv_cache, lengths, w_out):
    gathered = lax.all_gather(tokens, "yz", axis=0, tiled=True)
    sums = lax.psum(row_sums(gathered), "gx")
    normed = scale_rows(gathered, sums, gain)
    partial_qkv = jnp.dot(normed, w_qkv, preferred_element_type=jnp.float32)
    moved = lax.all_to_all(partial_qkv, "yz", split_axis=0, concat_axis=1, tiled=True)
    qkv = lax.psum_scatter(moved, "gx", scatter_dimension=0, tiled=True).astype(jnp.bfloat16)
    attended = attend(qkv, kv_cache, lengths)
    own_heads = lax.all_to_all(attended, "gx", split_axis=1, concat_axis=0, tiled=True)
    terms = jnp.dot(
        lax.all_gather(own_heads, "yz", axis=0, tiled=True),
        w_out,
        preferred_element_type=jnp.float32,
    )
    return lax.psum_scatter(terms, "gx", scatter_dimension=0, tiled=True).astype(jnp.bfloat16)


def solution(mesh):
    placed = (
        P(("ga", "yz"), "gx"),
        P("gx"),
        P("gx", "yz"),
        P(("ga", "yz", "gx"), None, None),
        P(("ga", "yz", "gx")),
        P("gx", "yz"),
    )
    return jax.shard_map(
        on_device, mesh=mesh, in_specs=placed, out_specs=P(("ga", "gx"), "yz"), check_vma=False
    )
```

profile of v0, /device:TPU:0, one launch (start us, length us, event | category | flops | bytes accessed | tf_op | source)
XLA Modules:
  0.0 136.8 jit_solution(4003664678934909719)
XLA Ops:
  6.5 0.0 copy-start.1
  6.5 0.0 copy-start
  6.5 32.9 %all-gather.1 = bf16[8,2,9216]{2,1,0:T(2,128)(2,1)S(1)} all-gather(bf16[1,2,9216]{2,1,0:T(2,128)(2,1)} %bitcast.35), channel_id=1, replica_groups=mesh['ga'=2,'gx'=2,'yz'=8] {'yz'}, dimensions={0}, use_global_device_ids=true | all-gather | bytes 331776 | tf_op jit(solution)/shard_map/all_gather | solution.py:49
  39.5 0.3 convert_reduce_fusion
  39.8 0.1 reshape.94
  39.9 0.1 reshape.95
  40.0 0.2 multiply_reduce_fusion
  40.1 2.5 %all-reduce.1 = (f32[16]{0:T(128)S(1)}, f32[16]{0:T(128)S(1)}) all-reduce(f32[16]{0:T(128)S(1)} %multiply_reduce_fusion, f32[16]{0:T(128)S(1)} %reshape.95), channel_id=1, replica_groups=mesh['ga'=2,'gx'=2,'yz'=8] {'gx'}, use_global_device_ids=true, to_apply=%region_3.0 | all-reduce | flops 32 | bytes 256 | tf_op jit(solution)/shard_map/psum | solution.py:50
  42.6 13.3 %fusion.3 = f32[16,1600]{1,0:T(8,128)S(1)} fusion(bf16[9216,1600]{0,1:T(8,128)(2,1)} %param.8, f32[16,9216]{1,0:T(8,128)S(1)} %reshape.94, f32[9216]{0:T(1024)} %param.7, f32[16]{0:T(128)S(1)} %get-tuple-element.10, f32[16]{0:T(128)S(1)} %get-tuple-element.9), kind=kOutput, calls=%fused_computation.8 | convolution fusion | flops 472449024 | bytes 30220416 | tf_op jit(solution)/shard_map/dot_general | solution.py:52
  56.0 0.7 all_to_all.26
  56.7 5.5 %all-to-all-start = ((f32[8,2,1600]{2,1,0:T(2,128)}), f32[8,2,1600]{2,1,0:T(2,128)S(1)}, u32[]{:S(2)}, u32[]{:S(2)}) async-start(f32[8,2,1600]{2,1,0:T(2,128)} %all_to_all.26), calls=%async_computation | async-start | bytes 212992 | tf_op jit(solution)/shard_map/all_to_all | solution.py:53
  62.2 0.0 reduce-scatter.2.cloned.1.call-start
  62.9 0.0 copy-done.1
  62.9 0.6 dynamic-slice
  63.5 5.9 %all-to-all-done = f32[8,2,1600]{2,1,0:T(2,128)S(1)} async-done(((f32[8,2,1600]{2,1,0:T(2,128)}), f32[8,2,1600]{2,1,0:T(2,128)S(1)}, u32[]{:S(2)}, u32[]{:S(2)}) %all-to-all-start) | async-done | bytes 102432 | tf_op jit(solution)/shard_map/all_to_all | solution.py:53
  69.4 0.1 all_to_all.29
  69.5 3.7 %all-reduce = bf16[2,12800]{1,0:T(2,128)(2,1)S(1)} all-reduce(f32[2,12800]{1,0:T(2,128)S(1)} %all_to_all.29), channel_id=3, replica_groups=mesh['ga'=2,'gx'=2,'yz'=8] {'gx'}, use_global_device_ids=true, to_apply=%region_4.0.clone | all-reduce | flops 25600 | bytes 153600
  73.3 0.7 dynamic-slice_convert_fusion
  74.0 0.1 slice_reduce_fusion
  74.2 0.0 copy-done
  74.2 0.3 fusion.21
  74.5 0.1 fusion.22
  74.6 0.2 fusion.14
  74.8 0.2 fusion.1
  75.1 0.5 broadcast.45
  75.6 0.8 reduce.8
  76.4 3.7 %all_to_all.36 = bf16[2,2,3072]{2,1,0:T(2,128)(2,1)S(1)} all-to-all(bf16[2,2,3072]{2,1,0:T(2,128)(2,1)S(1)} %reshape.101), channel_id=1, replica_groups=mesh['ga'=2,'gx'=2,'yz'=8] {'gx'}, dimensions={0} | all-to-all | bytes 49152 | tf_op jit(solution)/shard_map/all_to_all | solution.py:56
  80.2 31.3 %all-gather = bf16[1,16,6144]{2,0,1:T(2,128)(2,1)S(1)} all-gather(bf16[1,2,6144]{2,0,1:T(2,128)(2,1)S(1)} %bitcast.33), channel_id=2, replica_groups=mesh['ga'=2,'gx'=2,'yz'=8] {'yz'}, dimensions={1}, use_global_device_ids=true | all-gather | bytes 221184 | tf_op jit(solution)/shard_map/all_gather | solution.py:58
  111.5 11.7 %fusion.11 = f32[16,2304]{1,0:T(8,128)} fusion(bf16[6144,2304]{1,0:T(8,128)(2,1)} %param.11, bf16[1,16,6144]{2,0,1:T(2,128)(2,1)S(1)} %all-gather), kind=kOutput, calls=%fused_computation.16 | convolution fusion | flops 452984832 | bytes 28655616 | tf_op jit(solution)/shard_map/dot_general | solution.py:57
  123.2 0.0 reduce-scatter.2.cloned.1.call-update
  123.2 5.3 %reduce-scatter.2.cloned.1.call-done = f32[8,2304]{1,0:T(8,128)} async-done(((f32[16,2304]{1,0:T(8,128)}), f32[8,2304]{1,0:T(8,128)}) %reduce-scatter.2.cloned.1.call-update) | async-done | bytes 73744 | tf_op jit(solution)/shard_map/reduce_scatter | solution.py:62
  128.5 1.5 %convert_element_type.37 = bf16[8,2304]{1,0:T(8,128)(2,1)} convert(f32[8,2304]{1,0:T(8,128)} %reduce-scatter.2.cloned.1.call-done) | non-fusion elementwise | flops 18432 | bytes 110592 | tf_op jit(solution)/shard_map/convert_element_type | solution.py:62
  (9 shorter events, 0.1 us)
Async XLA Ops:
  6.5 56.4 %copy-start.1 = (u32[32]{0:T(128)S(1)}, u32[32]{0:T(128)}, u32[]{:S(2)}) copy-start(u32[32]{0:T(128)} %constant.22) | copy-start | bytes 388
  6.5 67.6 %copy-start = (bf16[1,512,512]{2,1,0:T(8,128)(2,1)S(1)}, bf16[1,512,512]{2,1,0:T(8,128)(2,1)}, u32[]{:S(2)}) copy-start(bf16[1,512,512]{2,1,0:T(8,128)(2,1)} %param.9) | copy-start | bytes 1572868
  56.7 12.7 %all-to-all-start = ((f32[8,2,1600]{2,1,0:T(2,128)}), f32[8,2,1600]{2,1,0:T(2,128)S(1)}, u32[]{:S(2)}, u32[]{:S(2)}) async-start(f32[8,2,1600]{2,1,0:T(2,128)} %all_to_all.26), calls=%async_computation | async-start | bytes 212992 | tf_op jit(solution)/shard_map/all_to_all | solution.py:53
  62.2 66.3 %reduce-scatter.2.cloned.1.call-start = ((), (), s32[]{:S(2)}) async-start(), calls=%async_computation.3 | async-start | bytes 221184 | tf_op jit(solution)/shard_map/reduce_scatter | solution.py:62
Sparse Core Ops, SparseCore 0:
  123.3 5.1 reduce-scatter.1
where the time goes:
time: 137 us
  blocking collectives  74.2 us (54%)
  matrix products  25.6 us (19%)
  between operations  14.1 us (10%)
  waiting for transfers between devices  11.2 us (8%)
  starting transfers between devices  5.58 us (4%)
  other arithmetic  3.06 us (2%)
  local copies, waits for them, and re-layouts  3.04 us (2%)
    all_gather x1, blocking collectives, on_device(): gathered = lax.all_gather(tokens, 'yz', axis=0, tiled=True)  32.9 us
    all_gather x1, blocking collectives, on_device(): lax.all_gather(own_heads, 'yz', axis=0, tiled=True)  31.3 us
    dot_general x1, matrix products, on_device(): partial_qkv = jnp.dot(normed, w_qkv, preferred_element_type=jnp.float32)  13.3 us
    dot_general x1, matrix products, on_device(): jnp.dot(lax.all_gather(own_heads, 'yz', axis=0, tiled=True), w_out, prefe...  11.7 us
    all_to_all x1, waiting for transfers between devices, on_device(): lax.all_to_all(partial_qkv, 'yz', split_axis=0, concat_axis=1, tiled=True)  5.88 us
    all_to_all x1, starting transfers between devices, on_device(): lax.all_to_all(partial_qkv, 'yz', split_axis=0, concat_axis=1, tiled=True)  5.54 us
    reduce_scatter x1, waiting for transfers between devices, on_device(): lax.psum_scatter(terms, 'gx', scatter_dimension=0, tiled=True)  5.32 us
    unnamed x1, blocking collectives  3.75 us
  transfers between devices with their start and end apart: 2, of which 2 were waited for; matrix products, arithmetic and copies ran while one was open for 0% of the time, Pallas kernels for 0%

commit v1 on v0

--- a/solution.py
+++ b/solution.py
@@ -45,24 +45,41 @@
     return attended.astype(jnp.bfloat16).reshape(seqs, HQ * HD)
 
 
-def on_device(tokens, gain, w_qkv, kv_cache, lengths, w_out):
-    gathered = lax.all_gather(tokens, "yz", axis=0, tiled=True)
-    sums = lax.psum(row_sums(gathered), "gx")
-    normed = scale_rows(gathered, sums, gain)
-    partial_qkv = jnp.dot(normed, w_qkv, preferred_element_type=jnp.float32)
-    moved = lax.all_to_all(partial_qkv, "yz", split_axis=0, concat_axis=1, tiled=True)
-    qkv = lax.psum_scatter(moved, "gx", scatter_dimension=0, tiled=True).astype(jnp.bfloat16)
-    attended = attend(qkv, kv_cache, lengths)
-    own_heads = lax.all_to_all(attended, "gx", split_axis=1, concat_axis=0, tiled=True)
-    terms = jnp.dot(
-        lax.all_gather(own_heads, "yz", axis=0, tiled=True),
-        w_out,
-        preferred_element_type=jnp.float32,
-    )
-    return lax.psum_scatter(terms, "gx", scatter_dimension=0, tiled=True).astype(jnp.bfloat16)
+def gather_rows(rows, axis, size):
+    copies = jnp.broadcast_to(rows[None], (size,) + rows.shape)
+    return lax.all_to_all(copies, axis, 0, 0, tiled=True).reshape(-1, rows.shape[-1])
+
+
+def make_on_device(groups, halves):
+    def on_device(tokens, gain, w_qkv, kv_cache, lengths, w_out):
+        own = lax.axis_index("gx")
+        sums = lax.psum(row_sums(tokens), "gx")
+        normed = gather_rows(scale_rows(tokens, sums, gain), "yz", groups)
+        partial_qkv = jnp.dot(normed, w_qkv, preferred_element_type=jnp.float32)
+        seqs = kv_cache.shape[0]
+        sent = partial_qkv.reshape(groups * halves, seqs, -1)
+        moved = lax.all_to_all(sent, ("yz", "gx"), 0, 0, tiled=True)
+        summed = moved.reshape(groups, halves, seqs, -1).sum(axis=1)
+        qkv = summed.astype(jnp.bfloat16).transpose(1, 0, 2).reshape(seqs, -1)
+        attended = attend(qkv, kv_cache, lengths)
+        by_half = attended.reshape(seqs, halves, -1).transpose(1, 0, 2)
+        sent = jnp.broadcast_to(by_half[None], (groups,) + by_half.shape)
+        sent = sent.reshape((groups * halves,) + by_half.shape[1:])
+        heads = lax.all_to_all(sent, ("yz", "gx"), 0, 0, tiled=True)
+        terms = jnp.dot(
+            heads.reshape(groups * halves * seqs, -1), w_out, preferred_element_type=jnp.float32
+        )
+        terms = terms.reshape(halves, -1, terms.shape[1])
+        kept = lax.dynamic_index_in_dim(terms, own, 0, keepdims=False)
+        given = lax.dynamic_index_in_dim(terms, 1 - own, 0, keepdims=False)
+        got = lax.ppermute(given, "gx", [(i, (i + 1) % halves) for i in range(halves)])
+        return (kept + got).astype(jnp.bfloat16)
+
+    return on_device
 
 
 def solution(mesh):
+    on_device = make_on_device(mesh.shape["yz"], mesh.shape["gx"])
     placed = (
         P(("ga", "yz"), "gx"),
         P("gx"),

time: 137 us -> 78.6 us (0.57)
  blocking collectives: 74.2 us -> 20.2 us
  between operations: 14.1 us -> 0.79 us
  waiting for transfers between devices: 11.2 us -> 17.1 us
  other arithmetic: 3.06 us -> 4.95 us
  starting transfers between devices: 5.58 us -> 7.1 us
    all_gather x2 -> x0, blocking collectives: 64.2 us -> none  [the longest x1 32.9 us: on_device(): gathered = lax.all_gather(tokens, 'yz', axis=0, tiled=True)]
    all_to_all x1, blocking collectives: 3.74 us -> 17.6 us  [gather_rows(): lax.all_to_all(copies, axis, 0, 0, tiled=True).reshape(-1, rows.shape[-1])]
    all_to_all x1 -> x2, waiting for transfers between devices: 5.88 us -> 15.8 us  [the longest x1 8.96 us: on_device(): heads = lax.all_to_all(sent, ('yz', 'gx'), 0, 0, tiled=True)]
    reduce_scatter x1 -> x0, waiting for transfers between devices: 5.32 us -> none  [on_device(): lax.psum_scatter(terms, 'gx', scatter_dimension=0, tiled=True)]
    unnamed x1 -> x0, blocking collectives: 3.75 us -> none
    broadcast_in_dim x0 -> x1, other arithmetic: none -> 1.76 us  [on_device(): sent = jnp.broadcast_to(by_half[None], (groups,) + by_half.shape)]
    all_to_all x1 -> x2, starting transfers between devices: 5.54 us -> 7.03 us  [the longest x1 3.52 us: on_device(): heads = lax.all_to_all(sent, ('yz', 'gx'), 0, 0, tiled=True)]
  transfers between devices with their start and end apart: 2 -> 3, of which waited for: 2 -> 3; matrix products, arithmetic and copies ran while one was open for 0% -> 0% of each run, Pallas kernels for 0% -> 0%
where the time goes in v1:
time: 78.6 us; the launch traced here: 78.1 us
  matrix products  24.9 us (32%)
  blocking collectives  20.2 us (26%)
  waiting for transfers between devices  17.1 us (22%)
  starting transfers between devices  7.1 us (9%)
  other arithmetic  4.95 us (6%)
  local copies, waits for them, and re-layouts  3.12 us (4%)
  between operations  0.79 us (1%)
    all_to_all x1, blocking collectives, gather_rows(): lax.all_to_all(copies, axis, 0, 0, tiled=True).reshape(-1, rows.shape[-1])  17.6 us
    dot_general x1, matrix products, on_device(): partial_qkv = jnp.dot(normed, w_qkv, preferred_element_type=jnp.float32)  13.3 us
    dot_general x1, matrix products, on_device(): jnp.dot(heads.reshape(groups * halves * seqs, -1), w_out, preferred_eleme...  11 us
    all_to_all x1, waiting for transfers between devices, on_device(): heads = lax.all_to_all(sent, ('yz', 'gx'), 0, 0, tiled=True)  8.96 us
    all_to_all x1, waiting for transfers between devices, on_device(): moved = lax.all_to_all(sent, ('yz', 'gx'), 0, 0, tiled=True)  6.84 us
    all_to_all x1, starting transfers between devices, on_device(): heads = lax.all_to_all(sent, ('yz', 'gx'), 0, 0, tiled=True)  3.52 us
    all_to_all x1, starting transfers between devices, on_device(): moved = lax.all_to_all(sent, ('yz', 'gx'), 0, 0, tiled=True)  3.51 us
    psum x1, blocking collectives, on_device(): sums = lax.psum(row_sums(tokens), 'gx')  2.59 us
  transfers between devices with their start and end apart: 3, of which 3 were waited for; matrix products, arithmetic and copies ran while one was open for 0% of the time, Pallas kernels for 0%

profile of v1, /device:TPU:0, one launch (start us, length us, event | category | flops | bytes accessed | tf_op | source)
XLA Modules:
  0.0 78.1 jit_solution(18318690496615898004)
XLA Ops:
  0.0 0.0 copy-start
  0.0 1.0 %convert_reduce_fusion = (f32[2]{0:T(128)S(1)}, f32[2]{0:T(128)S(1)}) fusion(bf16[2,9216]{1,0:T(2,128)(2,1)} %param.6), kind=kLoop, calls=%fused_computation.17 | loop fusion | flops 73724 | bytes 36880 | tf_op jit(solution)/shard_map/reduce_sum | solution.py:20
  1.0 2.6 %all-reduce = (f32[2]{0:T(128)S(1)}, f32[2]{0:T(128)S(1)}) all-reduce(f32[2]{0:T(128)S(1)} %get-tuple-element.6, f32[2]{0:T(128)S(1)} %get-tuple-element.5), channel_id=1, replica_groups=mesh['ga'=2,'gx'=2,'yz'=8] {'gx'}, use_global_device_ids=true, to_apply=%region_3.0 | all-reduce | flops 4 | bytes 32 | tf_op jit(solution)/shard_map/psum | solution.py:56
  3.6 0.9 %fusion.14 = bf16[2,9216]{1,0:T(2,128)(2,1)S(1)} fusion(bf16[2,9216]{1,0:T(2,128)(2,1)} %param.6, f32[2]{0:T(128)S(1)} %get-tuple-element.12, f32[2]{0:T(128)S(1)} %get-tuple-element.11, f32[9216]{0:T(1024)} %param.7), kind=kLoop, calls=%fused_computation.23 | loop fusion | flops 92160 | bytes 110608 | tf_op jit(solution)/shard_map/convert_element_type | solution.py:15
  4.6 0.2 broadcast_in_dim.43
  4.7 17.6 %all_to_all.15 = bf16[8,2,9216]{2,1,0:T(2,128)(2,1)S(1)} all-to-all(bf16[8,2,9216]{2,1,0:T(2,128)(2,1)S(1)} %broadcast_in_dim.43), channel_id=1, replica_groups=mesh['ga'=2,'gx'=2,'yz'=8] {'yz'}, dimensions={0} | all-to-all | bytes 589824 | tf_op jit(solution)/shard_map/all_to_all | solution.py:50
  22.3 0.1 reshape.111
  22.4 13.3 %convolution_bitcast_fusion = f32[16,1,1600]{2,0,1:T(8,128)S(1)} fusion(bf16[16,9216]{1,0:T(8,128)(2,1)S(1)} %reshape.111, bf16[9216,1600]{0,1:T(8,128)(2,1)} %param.8), kind=kOutput, calls=%fused_computation.2 | convolution fusion | flops 471859200 | bytes 29888512 | tf_op jit(solution)/shard_map/dot_general | solution.py:58
  35.7 0.8 copy.8
  36.5 3.5 %all-to-all-start.1 = ((f32[16,1,1600]{2,1,0:T(1,128)}), f32[16,1,1600]{2,1,0:T(1,128)S(1)}, u32[]{:S(2)}, u32[]{:S(2)}) async-start(f32[16,1,1600]{2,1,0:T(1,128)} %copy.8), calls=%async_computation.1 | async-start | bytes 212992 | tf_op jit(solution)/shard_map/all_to_all | solution.py:61
  40.7 6.8 %all-to-all-done.1 = f32[16,1,1600]{2,1,0:T(1,128)S(1)} async-done(((f32[16,1,1600]{2,1,0:T(1,128)}), f32[16,1,1600]{2,1,0:T(1,128)S(1)}, u32[]{:S(2)}, u32[]{:S(2)}) %all-to-all-start.1) | async-done | bytes 102432 | tf_op jit(solution)/shard_map/all_to_all | solution.py:61
  47.5 0.3 reduce.5
  47.8 0.1 reshape.113
  47.8 0.1 reduce_sum.38
  48.0 0.1 convert_element_type.45
  48.1 0.1 slice_reduce_fusion
  48.3 0.0 copy-done
  48.3 0.3 fusion.23
  48.6 0.1 fusion.24
  48.7 0.2 fusion.11
  48.9 0.2 fusion.3
  49.2 0.1 broadcast_in_dim.47
  49.3 0.2 broadcast_in_dim.49
  49.4 0.5 broadcast.50
  50.0 1.8 %reduce.8 = bf16[16,6144]{1,0:T(8,128)(2,1)S(1)} reduce(bf16[16,1,6144]{2,1,0:T(2,128)(2,1)S(1)} %broadcast_in_dim.49, bf16[]{:T(256)} %broadcast.50), dimensions={1}, to_apply=%broadcast_in_dim.49.reduce_sub_computation | reduce | bytes 393218 | tf_op jit(solution)/shard_map/broadcast_in_dim | solution.py:66
  51.7 0.8 %reshape.125 = bf16[16,2,3072]{2,1,0:T(2,128)(2,1)} reshape(bf16[16,6144]{1,0:T(8,128)(2,1)S(1)} %reduce.8) | data formatting | bytes 393216
  52.5 3.5 %all-to-all-start.2 = ((bf16[16,2,3072]{2,1,0:T(2,128)(2,1)}), bf16[16,2,3072]{2,1,0:T(2,128)(2,1)S(1)}, u32[]{:S(2)}, u32[]{:S(2)}) async-start(bf16[16,2,3072]{2,1,0:T(2,128)(2,1)} %reshape.125), calls=%async_computation.2 | async-start | bytes 393216 | tf_op jit(solution)/shard_map/all_to_all | solution.py:68
  56.1 9.0 %all-to-all-done.2 = bf16[16,2,3072]{2,1,0:T(2,128)(2,1)S(1)} async-done(((bf16[16,2,3072]{2,1,0:T(2,128)(2,1)}), bf16[16,2,3072]{2,1,0:T(2,128)(2,1)S(1)}, u32[]{:S(2)}, u32[]{:S(2)}) %all-to-all-start.2) | async-done | bytes 196640 | tf_op jit(solution)/shard_map/all_to_all | solution.py:68
  65.0 0.1 reshape.126
  65.2 11.0 %fusion = f32[2,8,2304]{2,1,0:T(8,128)S(1)} fusion(bf16[6144,2304]{1,0:T(8,128)(2,1)} %param.11, bf16[16,1,6144]{2,1,0:T(2,128)(2,1)S(1)} %reshape.126), kind=kOutput, calls=%fused_computation | convolution fusion | flops 452984832 | bytes 28655616 | tf_op jit(solution)/shard_map/dot_general | solution.py:69
  76.2 0.1 collective-permute-start
  76.3 1.3 %collective-permute-done = f32[8,2304]{1,0:T(8,128)S(1)} collective-permute-done((f32[8,2304]{1,0:T(8,128)S(1)}, f32[8,2304]{1,0:T(8,128)S(1)}, u32[]{:S(2)}, u32[]{:S(2)}) %collective-permute-start) | collective-permute-done | bytes 73760 | tf_op jit(solution)/shard_map/ppermute | solution.py:75
  77.5 0.6 fusion.16
  (7 shorter events, 0.1 us)
Async XLA Ops:
  0.0 48.3 %copy-start = (bf16[1,512,512]{2,1,0:T(8,128)(2,1)S(1)}, bf16[1,512,512]{2,1,0:T(8,128)(2,1)}, u32[]{:S(2)}) copy-start(bf16[1,512,512]{2,1,0:T(8,128)(2,1)} %param.9) | copy-start | bytes 1572868
  36.5 11.0 %all-to-all-start.1 = ((f32[16,1,1600]{2,1,0:T(1,128)}), f32[16,1,1600]{2,1,0:T(1,128)S(1)}, u32[]{:S(2)}, u32[]{:S(2)}) async-start(f32[16,1,1600]{2,1,0:T(1,128)} %copy.8), calls=%async_computation.1 | async-start | bytes 212992 | tf_op jit(solution)/shard_map/all_to_all | solution.py:61
  52.5 12.5 %all-to-all-start.2 = ((bf16[16,2,3072]{2,1,0:T(2,128)(2,1)}), bf16[16,2,3072]{2,1,0:T(2,128)(2,1)S(1)}, u32[]{:S(2)}, u32[]{:S(2)}) async-start(bf16[16,2,3072]{2,1,0:T(2,128)(2,1)} %reshape.125), calls=%async_computation.2 | async-start | bytes 393216 | tf_op jit(solution)/shard_map/all_to_all | solution.py:68
  76.2 1.3 %collective-permute-start = (f32[8,2304]{1,0:T(8,128)S(1)}, f32[8,2304]{1,0:T(8,128)S(1)}, u32[]{:S(2)}, u32[]{:S(2)}) collective-permute-start(f32[8,2304]{1,0:T(8,128)S(1)} %dynamic-slice_bitcast_fusion), channel_id=1, source_target_pairs={{0,8},{8,0},{1,9},{9,1},{2,10},{10,2},{3,11},{11,3},{4,12},{12,4},... | collective-permute-start | bytes 221192 | tf_op jit(solution)/shard_map/ppermute | solution.py:75

commit v2 on v0

v2 whole, which is shorter than its diff:
```python
import functools

import jax
import jax.numpy as jnp
from jax import lax
from jax.experimental import pallas as pl
from jax.experimental.pallas import tpu as pltpu
from jax.sharding import PartitionSpec as P

D = 18432
HQ = 48
HD = 256
MIB = 1 << 20
VMEM = pl.BlockSpec(memory_space=pltpu.VMEM)
ANY = pl.BlockSpec(memory_space=pl.ANY)
SMEM = pl.BlockSpec(memory_space=pltpu.SMEM)


def bytes_of(*shapes):
    total = 0
    for shape, width in shapes:
        size = width
        for dim in shape:
            size *= dim
        total += size
    return total


def spec_of(out):
    return VMEM if isinstance(out, jax.ShapeDtypeStruct) else ANY


def call(kernel, outs, in_specs, scratch, room, cost, *args):
    return pl.pallas_call(
        kernel,
        out_shape=outs,
        in_specs=in_specs,
        out_specs=jax.tree.map(spec_of, outs),
        scratch_shapes=scratch,
        compiler_params=pltpu.CompilerParams(vmem_limit_bytes=room + MIB),
        cost_estimate=pl.CostEstimate(flops=cost[0], bytes_accessed=cost[1], transcendentals=0),
    )(*args)


def sums_kernel(
    lengths_ref, tokens_hbm, gain_hbm, own_ref, gain_ref, sums_ref, used_ref, spare_hbm, own_sem, gain_sem
):
    own_copy = pltpu.make_async_copy(tokens_hbm, own_ref, own_sem)
    gain_copy = pltpu.make_async_copy(gain_hbm, gain_ref, gain_sem)
    own_copy.start()
    gain_copy.start()
    used_ref[...] = jnp.full(used_ref.shape, lengths_ref[0], jnp.int32)
    own_copy.wait()
    own = own_ref[...].astype(jnp.float32)
    lanes = sums_ref.shape[1:]
    sums_ref[0] = jnp.broadcast_to(jnp.sum(own, axis=1, keepdims=True), lanes)
    sums_ref[1] = jnp.broadcast_to(jnp.sum(own * own, axis=1, keepdims=True), lanes)
    gain_copy.wait()


def norm_kernel(own_ref, gain_ref, sums_ref, other_ref, spare_hbm, out_ref):
    total = sums_ref[0][:, 0:1] + other_ref[0][:, 0:1]
    squares = sums_ref[1][:, 0:1] + other_ref[1][:, 0:1]
    mean = total / D
    var = squares / D - mean * mean
    own = own_ref[...].astype(jnp.float32)
    normed = ((own - mean) * lax.rsqrt(var + 1e-06) * gain_ref[...]).astype(jnp.bfloat16)
    for i in range(out_ref.shape[0]):
        out_ref[i] = normed


def project_kernel(rows_ref, weight_ref, spare_hbm, out_ref, wide):
    groups, per, depth = rows_ref.shape
    for i in range(groups):
        wide[i * per : (i + 1) * per, :] = rows_ref[i].astype(jnp.float32)
    rows = wide[...].astype(jnp.bfloat16)
    terms = lax.dot_general(
        rows, weight_ref[...], (((1,), (1,)), ((), ())), preferred_element_type=jnp.float32
    )
    for i in range(out_ref.shape[0]):
        out_ref[i] = terms[i : i + 1, :]


def attend_kernel(halves, used_ref, parts_ref, cache_ref, spare_hbm, out_ref, heads):
    width = parts_ref.shape[2]
    pieces = []
    for i in range(parts_ref.shape[0] // halves):
        piece = parts_ref[i * halves]
        for j in range(1, halves):
            piece = piece + parts_ref[i * halves + j]
        pieces.append(piece)
    for h in range(HQ + 2):
        at = 0
        while at < HD:
            where = h * HD + at
            piece, start = where // width, where % width
            size = min(HD - at, width - start)
            heads[h : h + 1, at : at + size] = pieces[piece][:, start : start + size]
            at += size
    query = heads[0:HQ, :].astype(jnp.bfloat16)
    new = heads[HQ : HQ + 2, :].astype(jnp.bfloat16).astype(jnp.float32)
    cache = cache_ref[0]
    scores = (
        lax.dot_general(
            query, cache[:, :HD], (((1,), (1,)), ((), ())), preferred_element_type=jnp.float32
        )
        / 16.0
    )
    score_new = (
        jnp.sum(query.astype(jnp.float32) * new[0:1, :], axis=1, keepdims=True) / 16.0
    )
    valid = lax.broadcasted_iota(jnp.int32, scores.shape, 1) < used_ref[0:1, 0:1]
    masked = jnp.where(valid, scores, -1e30)
    top = jnp.maximum(jnp.max(masked, axis=1, keepdims=True), score_new)
    expd = jnp.where(valid, jnp.exp(masked - top), 0.0)
    exp_new = jnp.exp(score_new - top)
    total = jnp.sum(expd, axis=1, keepdims=True) + exp_new
    probs = (expd / total).astype(jnp.bfloat16)
    prob_new = (exp_new / total).astype(jnp.bfloat16).astype(jnp.float32)
    attended = jnp.dot(probs, cache[:, HD:], preferred_element_type=jnp.float32)
    attended = (attended + prob_new * new[1:2, :]).astype(jnp.bfloat16)
    per = HQ // halves
    for i in range(out_ref.shape[0]):
        j = i % halves
        out_ref[i] = attended[j * per : (j + 1) * per, :]


def output_kernel(halves, attended_ref, weight_ref, kept_ref, given_ref, wide, rows):
    seqs, per, depth = attended_ref.shape
    lanes = wide.shape[2]
    for c in range(depth // lanes):
        part = attended_ref[:, :, c * lanes : (c + 1) * lanes].astype(jnp.float32)
        wide[c] = part.reshape(seqs * per, lanes)
        for h in range(per):
            at = h * depth + c * lanes
            rows[:, at : at + lanes] = wide[c, pl.ds(h, seqs, stride=per), :].astype(jnp.bfloat16)
    terms = jnp.dot(rows[...], weight_ref[...], preferred_element_type=jnp.float32)
    own = lax.axis_index("gx")
    size = seqs // halves

    @pl.when(own == 0)
    def _():
        kept_ref[...] = terms[:size]
        given_ref[...] = terms[size:]

    @pl.when(own != 0)
    def _():
        kept_ref[...] = terms[size:]
        given_ref[...] = terms[:size]


def make_on_device(groups, halves):
    swap = [(i, (i + 1) % halves) for i in range(halves)]

    def on_device(tokens, gain, w_qkv, kv_cache, lengths, w_out):
        f32, bf16 = jnp.float32, jnp.bfloat16
        members = groups * halves
        per, depth = tokens.shape
        width = w_qkv.shape[1]
        wide_out = w_out.shape[1]
        batch = groups * per
        w_in = pltpu.with_memory_space_constraint(w_qkv.T, pltpu.VMEM)
        w_back = pltpu.with_memory_space_constraint(w_out, pltpu.VMEM)

        own, scale, sums, used, spare = call(
            sums_kernel,
            [
                jax.ShapeDtypeStruct((per, depth), bf16),
                jax.ShapeDtypeStruct((1, depth), f32),
                jax.ShapeDtypeStruct((2, per, 128), f32),
                jax.ShapeDtypeStruct((8, 128), jnp.int32),
                pltpu.HBM((2 * depth * width // 1024, 1024), bf16),
            ],
            [SMEM, ANY, ANY],
            [pltpu.SemaphoreType.DMA, pltpu.SemaphoreType.DMA],
            bytes_of(((8, depth), 12)),
            (4 * per * depth, 2 * per * depth),
            lengths,
            pltpu.with_memory_space_constraint(tokens, pltpu.HBM),
            pltpu.with_memory_space_constraint(gain.reshape(1, -1), pltpu.HBM),
        )
        spare = pltpu.with_memory_space_constraint(spare, pltpu.HBM)
        other = lax.ppermute(sums, "gx", swap)
        normed = call(
            norm_kernel,
            jax.ShapeDtypeStruct((groups, per, depth), bf16),
            [VMEM, VMEM, VMEM, VMEM, ANY],
            [],
            bytes_of(((groups, per, depth), 2), ((8, depth), 12)),
            (6 * per * depth, 2 * groups * per * depth),
            own,
            scale,
            sums,
            other,
            spare,
        )
        rows = lax.all_to_all(normed, "yz", 0, 0, tiled=True)
        parts = call(
            project_kernel,
            jax.ShapeDtypeStruct((members, 1, width), f32),
            [VMEM, VMEM, ANY],
            [pltpu.VMEM((batch, depth), f32)],
            bytes_of(((batch, depth), 8), ((batch, width + 128), 16)),
            (2 * batch * depth * width, depth * width * 2),
            rows,
            w_in,
            spare,
        )
        moved = lax.all_to_all(parts, ("yz", "gx"), 0, 0, tiled=True)
        attended = call(
            functools.partial(attend_kernel, halves),
            jax.ShapeDtypeStruct((members, HQ // halves, HD), bf16),
            [VMEM, VMEM, VMEM, ANY],
            [pltpu.VMEM((HQ + 8, HD), f32)],
            bytes_of(((members, HQ // halves, HD), 4), ((512, 512), 4), ((members, 8, width + 128), 8)),
            (4 * HQ * 512 * HD, w_out.shape[0] * wide_out * 2),
            used,
            moved,
            kv_cache,
            spare,
        )
        gathered = lax.all_to_all(attended, ("yz", "gx"), 0, 0, tiled=True)
        size = batch // halves
        kept, given = call(
            functools.partial(output_kernel, halves),
            [jax.ShapeDtypeStruct((size, wide_out), f32)] * 2,
            [VMEM, VMEM],
            [
                pltpu.VMEM((HD // 128, batch * (HQ // halves), 128), f32),
                pltpu.VMEM((batch, HQ // halves * HD), bf16),
            ],
            bytes_of(((batch, HQ // halves, HD), 10), ((batch, wide_out + 128), 12)),
            (2 * batch * w_out.shape[0] * wide_out, w_out.shape[0] * wide_out * 2),
            gathered,
            w_back,
        )
        got = lax.ppermute(given, "gx", swap)
        return (kept + got).astype(bf16)

    return on_device


def solution(mesh):
    placed = (
        P(("ga", "yz"), "gx"),
        P("gx"),
        P("gx", "yz"),
        P(("ga", "yz", "gx"), None, None),
        P(("ga", "yz", "gx")),
        P("gx", "yz"),
    )
    return jax.shard_map(
        make_on_device(mesh.shape["yz"], mesh.shape["gx"]),
        mesh=mesh,
        in_specs=placed,
        out_specs=P(("ga", "gx"), "yz"),
        check_vma=False,
    )
```

time: 137 us -> 57.6 us (0.42)
  blocking collectives: 74.2 us -> 40.2 us
  matrix products: 25.6 us -> 0 us
  between operations: 14.1 us -> 0.76 us
  Pallas kernels: 0 us -> 13.2 us
  waiting for transfers between devices: 11.2 us -> 2.09 us
  starting transfers between devices: 5.58 us -> 0.52 us
  local copies, waits for them, and re-layouts: 3.04 us -> 0.04 us
  other arithmetic: 3.06 us -> 0.63 us
    all_gather x2 -> x0, blocking collectives: 64.2 us -> none  [the longest x1 32.9 us: on_device(): gathered = lax.all_gather(tokens, 'yz', axis=0, tiled=True)]
    all_to_all x1 -> x3, blocking collectives: 3.74 us -> 40.2 us  [the longest x1 17.9 us: on_device(): rows = lax.all_to_all(normed, 'yz', 0, 0, tiled=True)]
    dot_general x5 -> x0, matrix products: 25.6 us -> none  [the longest x1 13.3 us: on_device(): partial_qkv = jnp.dot(normed, w_qkv, preferred_element_type=jnp.float32)]
    pallas_call x0 -> x5, Pallas kernels: none -> 13.2 us  [call(): pl.pallas_call(kernel, out_shape=outs, in_specs=in_specs, out_specs=jax.t...]
    all_to_all x1 -> x0, waiting for transfers between devices: 5.88 us -> none  [on_device(): lax.all_to_all(partial_qkv, 'yz', split_axis=0, concat_axis=1, tiled=True)]
    all_to_all x1 -> x0, starting transfers between devices: 5.54 us -> none  [on_device(): lax.all_to_all(partial_qkv, 'yz', split_axis=0, concat_axis=1, tiled=True)]
    reduce_scatter x1 -> x0, waiting for transfers between devices: 5.32 us -> none  [on_device(): lax.psum_scatter(terms, 'gx', scatter_dimension=0, tiled=True)]
    unnamed x1 -> x0, blocking collectives: 3.75 us -> none
where the time goes in v2:
time: 57.6 us; the launch traced here: 57.4 us
  blocking collectives  40.2 us (70%)
  Pallas kernels  13.2 us (23%)
  waiting for transfers between devices  2.09 us (4%)
  between operations  0.76 us (1%)
  other arithmetic  0.63 us (1%)
    all_to_all x1, blocking collectives, on_device(): rows = lax.all_to_all(normed, 'yz', 0, 0, tiled=True)  17.9 us
    pallas_call x5, Pallas kernels, call(): pl.pallas_call(kernel, out_shape=outs, in_specs=in_specs, out_specs=jax.t...  13.2 us
    all_to_all x1, blocking collectives, on_device(): gathered = lax.all_to_all(attended, ('yz', 'gx'), 0, 0, tiled=True)  12 us
    all_to_all x1, blocking collectives, on_device(): moved = lax.all_to_all(parts, ('yz', 'gx'), 0, 0, tiled=True)  10.3 us
    ppermute x1, waiting for transfers between devices, on_device(): got = lax.ppermute(given, 'gx', swap)  1.27 us
  transfers between devices with their start and end apart: 2, of which 2 were waited for; matrix products, arithmetic and copies ran while one was open for 0% of the time, Pallas kernels for 0%

profile of v2, /device:TPU:0, one launch (start us, length us, event | category | flops | bytes accessed | tf_op | source)
XLA Modules:
  0.0 57.4 jit_solution(4809100315776264030)
XLA Ops:
  0.7 1.0 %shard_map.64 = (bf16[2,9216]{1,0:T(2,128)(2,1)S(1)}, f32[1,9216]{1,0:T(1,128)S(1)}, f32[2,2,128]{2,1,0:T(2,128)S(1)}, s32[8,128]{1,0:T(8,128)S(1)}, bf16[28800,1024]{1,0:T(8,128)(2,1)}) custom-call(s32[1]{0:T(128)S(6)} %copy.7.lengths_ref, bf16[2,9216]{1,0:T(2,128)(2,1)} %tokens_hbm.1, f32[1,9216]{1,0:T(1,128)} %bitcast.5), custom_call_target="tpu_custom_call" | custom-call | flops 73728 | bytes 36864 | tf_op jit(solution)/shard_map/pallas_call | solution.py:34
  1.6 0.5 collective-permute-start
  2.1 0.8 %collective-permute-done.other_ref = f32[2,2,128]{2,1,0:T(2,128)S(1)} collective-permute-done((f32[2,2,128]{2,1,0:T(2,128)S(1)}, f32[2,2,128]{2,1,0:T(2,128)S(1)}, u32[]{:S(2)}, u32[]{:S(2)}) %collective-permute-start) | collective-permute-done | bytes 2080 | tf_op jit(solution)/shard_map/ppermute | solution.py:183
  3.0 0.0 copy-start
  3.0 0.1 shard_map.65
  3.1 17.9 %all_to_all.15.rows_ref = bf16[8,2,9216]{2,1,0:T(2,128)(2,1)S(1)} all-to-all(bf16[8,2,9216]{2,1,0:T(2,128)(2,1)S(1)} %shard_map.65), channel_id=1, replica_groups=mesh['ga'=2,'gx'=2,'yz'=8] {'yz'}, dimensions={0} | all-to-all | bytes 589824 | tf_op jit(solution)/shard_map/all_to_all | solution.py:197
  21.0 0.0 copy-done
  21.0 0.0 copy-start.1
  21.0 0.0 slice-start
  21.0 0.0 slice-start.1
  21.0 0.0 slice-start.2
  21.0 0.0 slice-start.3
  21.0 0.0 slice-start.4
  21.0 7.8 %shard_map.66 = f32[16,1,1600]{2,1,0:T(1,128)S(1)} custom-call(bf16[8,2,9216]{2,1,0:T(2,128)(2,1)S(1)} %all_to_all.15.rows_ref, bf16[1600,9216]{1,0:T(8,128)(2,1)S(1)} %bitcast.2, bf16[28800,1024]{1,0:T(8,128)(2,1)} %get-tuple-element.16.spare_hbm), custom_call_target="tpu_custom_call" | custom-call | flops 471859200 | bytes 29491200 | tf_op jit(solution)/shard_map/pallas_call | solution.py:34
  28.8 10.3 %all_to_all.16.parts_ref = f32[16,1,1600]{2,1,0:T(1,128)S(1)} all-to-all(f32[16,1,1600]{2,1,0:T(1,128)S(1)} %shard_map.66), channel_id=1, replica_groups=mesh['ga'=2,'gx'=2,'yz'=8] {'yz','gx'}, dimensions={0} | all-to-all | bytes 204800 | tf_op jit(solution)/shard_map/all_to_all | solution.py:209
  39.1 0.0 copy-done.1
  39.1 0.0 slice-start.5
  39.1 0.0 slice-start.6
  39.1 0.5 shard_map.67
  39.6 12.0 %all_to_all.17.attended_ref = bf16[16,24,256]{2,1,0:T(8,128)(2,1)S(1)} all-to-all(bf16[16,24,256]{2,1,0:T(8,128)(2,1)S(1)} %shard_map.67), channel_id=1, replica_groups=mesh['ga'=2,'gx'=2,'yz'=8] {'yz','gx'}, dimensions={0} | all-to-all | bytes 393216 | tf_op jit(solution)/shard_map/all_to_all | solution.py:222
  51.6 0.0 slice-done
  51.6 0.0 slice-done.1
  51.6 0.0 slice-done.2
  51.6 0.0 slice-done.3
  51.6 0.0 slice-done.4
  51.7 0.0 slice-done.5
  51.7 0.0 slice-done.6
  51.7 3.8 %shard_map.68 = (f32[8,2304]{1,0:T(8,128)S(1)}, f32[8,2304]{1,0:T(8,128)S(1)}) custom-call(bf16[16,24,256]{2,1,0:T(8,128)(2,1)S(1)} %all_to_all.17.attended_ref, bf16[6144,2304]{1,0:T(8,128)(2,1)S(1)} %bitcast.4), custom_call_target="tpu_custom_call" | custom-call | flops 452984832 | bytes 28311552 | tf_op jit(solution)/shard_map/pallas_call | solution.py:34
  55.5 0.0 collective-permute-start.1
  55.5 1.3 %collective-permute-done.1 = f32[8,2304]{1,0:T(8,128)S(1)} collective-permute-done((f32[8,2304]{1,0:T(8,128)S(1)}, f32[8,2304]{1,0:T(8,128)S(1)}, u32[]{:S(2)}, u32[]{:S(2)}) %collective-permute-start.1) | collective-permute-done | bytes 73760 | tf_op jit(solution)/shard_map/ppermute | solution.py:237
  56.8 0.6 %add_convert_fusion = bf16[8,2304]{1,0:T(8,128)(2,1)} fusion(f32[8,2304]{1,0:T(8,128)S(1)} %get-tuple-element.17, f32[8,2304]{1,0:T(8,128)S(1)} %collective-permute-done.1), kind=kLoop, calls=%fused_computation | loop fusion | flops 36864 | bytes 184320 | tf_op jit(solution)/shard_map/convert_element_type | solution.py:238
  (1 shorter events, 0.0 us)
Async XLA Ops:
  1.6 1.3 %collective-permute-start = (f32[2,2,128]{2,1,0:T(2,128)S(1)}, f32[2,2,128]{2,1,0:T(2,128)S(1)}, u32[]{:S(2)}, u32[]{:S(2)}) collective-permute-start(f32[2,2,128]{2,1,0:T(2,128)S(1)} %get-tuple-element.15.sums_ref), channel_id=1, source_target_pairs={{0,8},{8,0},{1,9},{9,1},{2,10},{10,2},{3,11},{11,3},{4,12},{12,4},... | collective-permute-start | bytes 6152 | tf_op jit(solution)/shard_map/ppermute | solution.py:183
  3.0 18.0 %copy-start = (bf16[9216,1600]{0,1:T(8,128)(2,1)S(1)}, bf16[9216,1600]{0,1:T(8,128)(2,1)}, u32[]{:S(2)}) copy-start(bf16[9216,1600]{0,1:T(8,128)(2,1)} %param.8) | copy-start | bytes 88473600
  21.0 18.1 %copy-start.1 = (bf16[1,512,512]{2,1,0:T(8,128)(2,1)S(1)}, bf16[1,512,512]{2,1,0:T(8,128)(2,1)}, u32[]{:S(2)}) copy-start(bf16[1,512,512]{2,1,0:T(8,128)(2,1)} %cache_ref.1) | copy-start | bytes 1572868
  21.0 30.7 %slice-start = ((s8[28311552]{0:T(1024)(128)(4,1)}), s8[3145728]{0:T(1024)(128)(4,1)S(1)}, s32[]{:S(2)}) async-start(s8[28311552]{0:T(1024)(128)(4,1)} %bitcast.3), calls=%async_computation.3 | async-start | bytes 6291456
  21.0 30.7 %slice-start.1 = ((s8[28311552]{0:T(1024)(128)(4,1)}), s8[4194304]{0:T(1024)(128)(4,1)S(1)}, s32[]{:S(2)}) async-start(s8[28311552]{0:T(1024)(128)(4,1)} %bitcast.3), calls=%async_computation.4 | async-start | bytes 8388608
  21.0 30.6 %slice-start.2 = ((s8[28311552]{0:T(1024)(128)(4,1)}), s8[4194304]{0:T(1024)(128)(4,1)S(1)}, s32[]{:S(2)}) async-start(s8[28311552]{0:T(1024)(128)(4,1)} %bitcast.3), calls=%async_computation.5 | async-start | bytes 8388608
  21.0 30.6 %slice-start.3 = ((s8[28311552]{0:T(1024)(128)(4,1)}), s8[4194304]{0:T(1024)(128)(4,1)S(1)}, s32[]{:S(2)}) async-start(s8[28311552]{0:T(1024)(128)(4,1)} %bitcast.3), calls=%async_computation.6 | async-start | bytes 8388608
  21.0 30.6 %slice-start.4 = ((s8[28311552]{0:T(1024)(128)(4,1)}), s8[4194304]{0:T(1024)(128)(4,1)S(1)}, s32[]{:S(2)}) async-start(s8[28311552]{0:T(1024)(128)(4,1)} %bitcast.3), calls=%async_computation.7 | async-start | bytes 8388608
  39.1 12.5 %slice-start.5 = ((s8[28311552]{0:T(1024)(128)(4,1)}), s8[4194304]{0:T(1024)(128)(4,1)S(1)}, s32[]{:S(2)}) async-start(s8[28311552]{0:T(1024)(128)(4,1)} %bitcast.3), calls=%async_computation.8 | async-start | bytes 8388608
  39.1 12.6 %slice-start.6 = ((s8[28311552]{0:T(1024)(128)(4,1)}), s8[4194304]{0:T(1024)(128)(4,1)S(1)}, s32[]{:S(2)}) async-start(s8[28311552]{0:T(1024)(128)(4,1)} %bitcast.3), calls=%async_computation.9 | async-start | bytes 8388608
  55.5 1.3 %collective-permute-start.1 = (f32[8,2304]{1,0:T(8,128)S(1)}, f32[8,2304]{1,0:T(8,128)S(1)}, u32[]{:S(2)}, u32[]{:S(2)}) collective-permute-start(f32[8,2304]{1,0:T(8,128)S(1)} %get-tuple-element.18), channel_id=1, source_target_pairs={{0,8},{8,0},{1,9},{9,1},{2,10},{10,2},{3,11},{11,3},{4,12},{12,4},... | collective-permute-start | bytes 221192 | tf_op jit(solution)/shard_map/ppermute | solution.py:237

commit v3 on v2

--- a/solution.py
+++ b/solution.py
@@ -12,8 +12,8 @@
 HD = 256
 MIB = 1 << 20
 VMEM = pl.BlockSpec(memory_space=pltpu.VMEM)
+SMEM = pl.BlockSpec(memory_space=pltpu.SMEM)
 ANY = pl.BlockSpec(memory_space=pl.ANY)
-SMEM = pl.BlockSpec(memory_space=pltpu.SMEM)
 
 
 def bytes_of(*shapes):
@@ -42,46 +42,57 @@
     )(*args)
 
 
-def sums_kernel(
-    lengths_ref, tokens_hbm, gain_hbm, own_ref, gain_ref, sums_ref, used_ref, spare_hbm, own_sem, gain_sem
+def load_kernel(
+    lengths_ref, tokens_hbm, gain_hbm, own_ref, gain_ref, used_ref, spare_hbm, sems
 ):
-    own_copy = pltpu.make_async_copy(tokens_hbm, own_ref, own_sem)
-    gain_copy = pltpu.make_async_copy(gain_hbm, gain_ref, gain_sem)
-    own_copy.start()
-    gain_copy.start()
+    copies = [
+        pltpu.make_async_copy(tokens_hbm, own_ref, sems.at[0]),
+        pltpu.make_async_copy(gain_hbm, gain_ref, sems.at[1]),
+    ]
+    for copy in copies:
+        copy.start()
     used_ref[...] = jnp.full(used_ref.shape, lengths_ref[0], jnp.int32)
-    own_copy.wait()
-    own = own_ref[...].astype(jnp.float32)
-    lanes = sums_ref.shape[1:]
-    sums_ref[0] = jnp.broadcast_to(jnp.sum(own, axis=1, keepdims=True), lanes)
-    sums_ref[1] = jnp.broadcast_to(jnp.sum(own * own, axis=1, keepdims=True), lanes)
-    gain_copy.wait()
-
-
-def norm_kernel(own_ref, gain_ref, sums_ref, other_ref, spare_hbm, out_ref):
-    total = sums_ref[0][:, 0:1] + other_ref[0][:, 0:1]
-    squares = sums_ref[1][:, 0:1] + other_ref[1][:, 0:1]
-    mean = total / D
-    var = squares / D - mean * mean
-    own = own_ref[...].astype(jnp.float32)
-    normed = ((own - mean) * lax.rsqrt(var + 1e-06) * gain_ref[...]).astype(jnp.bfloat16)
-    for i in range(out_ref.shape[0]):
+    for copy in copies:
+        copy.wait()
+
+
+def sums_kernel(rows_refs, sums_ref):
+    for i, ref in enumerate(rows_refs):
+        rows = ref[...].astype(jnp.float32)
+        lanes = sums_ref.shape[2:]
+        sums_ref[i, 0] = jnp.broadcast_to(jnp.sum(rows, axis=1, keepdims=True), lanes)
+        sums_ref[i, 1] = jnp.broadcast_to(jnp.sum(rows * rows, axis=1, keepdims=True), lanes)
+
+
+def norm_kernel(rows_refs, gain_ref, sums_ref, other_ref, spare_hbm, out_ref):
+    for i, ref in enumerate(rows_refs):
+        total = sums_ref[i, 0][:, 0:1] + other_ref[i, 0][:, 0:1]
+        squares = sums_ref[i, 1][:, 0:1] + other_ref[i, 1][:, 0:1]
+        mean = total / D
+        var = squares / D - mean * mean
+        rows = ref[...].astype(jnp.float32)
+        normed = ((rows - mean) * lax.rsqrt(var + 1e-06) * gain_ref[...]).astype(jnp.bfloat16)
         out_ref[i] = normed
 
 
-def project_kernel(rows_ref, weight_ref, spare_hbm, out_ref, wide):
-    groups, per, depth = rows_ref.shape
-    for i in range(groups):
-        wide[i * per : (i + 1) * per, :] = rows_ref[i].astype(jnp.float32)
+def project_kernel(order, block_refs, weight_ref, out_ref, wide):
+    group = lax.axis_index("yz")
+    at, places = 0, []
+    for ref, origins in zip(block_refs, order):
+        per = ref.shape[1]
+        for i, origin in enumerate(origins):
+            wide[at : at + per, :] = ref[i].astype(jnp.float32)
+            places.extend(origin(group) * per + r for r in range(per))
+            at += per
     rows = wide[...].astype(jnp.bfloat16)
     terms = lax.dot_general(
         rows, weight_ref[...], (((1,), (1,)), ((), ())), preferred_element_type=jnp.float32
     )
-    for i in range(out_ref.shape[0]):
-        out_ref[i] = terms[i : i + 1, :]
-
-
-def attend_kernel(halves, used_ref, parts_ref, cache_ref, spare_hbm, out_ref, heads):
+    for i, place in enumerate(places):
+        out_ref[place] = terms[i : i + 1, :]
+
+
+def attend_kernel(halves, used_ref, parts_ref, cache_ref, spare_refs, out_ref, heads):
     width = parts_ref.shape[2]
     pieces = []
     for i in range(parts_ref.shape[0] // halves):
@@ -152,6 +163,9 @@
 def make_on_device(groups, halves):
     swap = [(i, (i + 1) % halves) for i in range(halves)]
 
+    def pairs(k):
+        return [(i, i ^ k) for i in range(groups)]
+
     def on_device(tokens, gain, w_qkv, kv_cache, lengths, w_out):
         f32, bf16 = jnp.float32, jnp.bfloat16
         members = groups * halves
@@ -162,62 +176,73 @@
         w_in = pltpu.with_memory_space_constraint(w_qkv.T, pltpu.VMEM)
         w_back = pltpu.with_memory_space_constraint(w_out, pltpu.VMEM)
 
-        own, scale, sums, used, spare = call(
-            sums_kernel,
+        own, scale, used, spare = call(
+            load_kernel,
             [
                 jax.ShapeDtypeStruct((per, depth), bf16),
                 jax.ShapeDtypeStruct((1, depth), f32),
-                jax.ShapeDtypeStruct((2, per, 128), f32),
                 jax.ShapeDtypeStruct((8, 128), jnp.int32),
                 pltpu.HBM((2 * depth * width // 1024, 1024), bf16),
             ],
             [SMEM, ANY, ANY],
-            [pltpu.SemaphoreType.DMA, pltpu.SemaphoreType.DMA],
-            bytes_of(((8, depth), 12)),
-            (4 * per * depth, 2 * per * depth),
+            [pltpu.SemaphoreType.DMA((2,))],
+            bytes_of(((8, depth), 8)),
+            (per * depth, 2 * per * depth),
             lengths,
             pltpu.with_memory_space_constraint(tokens, pltpu.HBM),
             pltpu.with_memory_space_constraint(gain.reshape(1, -1), pltpu.HBM),
         )
         spare = pltpu.with_memory_space_constraint(spare, pltpu.HBM)
+        mate = lax.ppermute(tokens, "yz", pairs(1))
+        sums = call(
+            sums_kernel,
+            jax.ShapeDtypeStruct((2, 2, per, 128), f32),
+            [[VMEM, VMEM]],
+            [],
+            bytes_of(((8, depth), 8)),
+            (8 * per * depth, 4 * per * depth),
+            [own, mate],
+        )
         other = lax.ppermute(sums, "gx", swap)
         normed = call(
             norm_kernel,
-            jax.ShapeDtypeStruct((groups, per, depth), bf16),
-            [VMEM, VMEM, VMEM, VMEM, ANY],
+            jax.ShapeDtypeStruct((2, per, depth), bf16),
+            [[VMEM, VMEM], VMEM, VMEM, VMEM, ANY],
             [],
-            bytes_of(((groups, per, depth), 2), ((8, depth), 12)),
-            (6 * per * depth, 2 * groups * per * depth),
-            own,
+            bytes_of(((8, depth), 24)),
+            (12 * per * depth, 4 * per * depth),
+            [own, mate],
             scale,
             sums,
             other,
             spare,
         )
-        rows = lax.all_to_all(normed, "yz", 0, 0, tiled=True)
+        blocks = [normed] + [lax.ppermute(normed, "yz", pairs(k)) for k in range(2, groups, 2)]
+        order = [
+            [lambda g, k=k: g ^ k, lambda g, k=k: g ^ k ^ 1] for k in range(0, groups, 2)
+        ]
         parts = call(
-            project_kernel,
+            functools.partial(project_kernel, order),
             jax.ShapeDtypeStruct((members, 1, width), f32),
-            [VMEM, VMEM, ANY],
+            [[VMEM] * len(blocks), VMEM],
             [pltpu.VMEM((batch, depth), f32)],
             bytes_of(((batch, depth), 8), ((batch, width + 128), 16)),
             (2 * batch * depth * width, depth * width * 2),
-            rows,
+            blocks,
             w_in,
-            spare,
         )
         moved = lax.all_to_all(parts, ("yz", "gx"), 0, 0, tiled=True)
         attended = call(
             functools.partial(attend_kernel, halves),
             jax.ShapeDtypeStruct((members, HQ // halves, HD), bf16),
-            [VMEM, VMEM, VMEM, ANY],
+            [VMEM, VMEM, VMEM, [ANY] * 4],
             [pltpu.VMEM((HQ + 8, HD), f32)],
             bytes_of(((members, HQ // halves, HD), 4), ((512, 512), 4), ((members, 8, width + 128), 8)),
             (4 * HQ * 512 * HD, w_out.shape[0] * wide_out * 2),
             used,
             moved,
             kv_cache,
-            spare,
+            [spare] * 4,
         )
         gathered = lax.all_to_all(attended, ("yz", "gx"), 0, 0, tiled=True)
         size = batch // halves

time: 57.6 us -> 56.1 us (0.974)
  blocking collectives: 40.2 us -> 24.4 us
  starting transfers between devices: 0.52 us -> 7.78 us
  waiting for transfers between devices: 2.09 us -> 8.98 us
    all_to_all x1 -> x0, blocking collectives: 17.9 us -> none  [on_device(): rows = lax.all_to_all(normed, 'yz', 0, 0, tiled=True)]
    ppermute x0 -> x4, starting transfers between devices: none -> 7.78 us  [the longest x3 4.84 us: on_device(): lax.ppermute(normed, 'yz', pairs(k))]
    ppermute x0 -> x4, waiting for transfers between devices: none -> 6.54 us  [the longest x3 5.86 us: on_device(): lax.ppermute(normed, 'yz', pairs(k))]
    all_to_all x1, blocking collectives: 10.3 us -> 12.3 us  [on_device(): moved = lax.all_to_all(parts, ('yz', 'gx'), 0, 0, tiled=True)]
    pallas_call x5 -> x6, Pallas kernels: 13.2 us -> 13.3 us  [call(): pl.pallas_call(kernel, out_shape=outs, in_specs=in_specs, out_specs=jax.t...]
  transfers between devices with their start and end apart: 2 -> 6, of which waited for: 2 -> 5; matrix products, arithmetic and copies ran while one was open for 0% -> 0% of each run, Pallas kernels for 0% -> 1%
where the time goes in v3:
time: 56.1 us; the launch traced here: 55.9 us
  blocking collectives  24.4 us (43%)
  Pallas kernels  13.3 us (24%)
  waiting for transfers between devices  8.98 us (16%)
  starting transfers between devices  7.78 us (14%)
  between operations  0.77 us (1%)
  other arithmetic  0.63 us (1%)
    pallas_call x6, Pallas kernels, call(): pl.pallas_call(kernel, out_shape=outs, in_specs=in_specs, out_specs=jax.t...  13.3 us
    all_to_all x1, blocking collectives, on_device(): moved = lax.all_to_all(parts, ('yz', 'gx'), 0, 0, tiled=True)  12.3 us
    all_to_all x1, blocking collectives, on_device(): gathered = lax.all_to_all(attended, ('yz', 'gx'), 0, 0, tiled=True)  12.1 us
    ppermute x3, waiting for transfers between devices, on_device(): lax.ppermute(normed, 'yz', pairs(k))  5.86 us
    ppermute x3, starting transfers between devices, on_device(): lax.ppermute(normed, 'yz', pairs(k))  4.84 us
    ppermute x1, starting transfers between devices, on_device(): mate = lax.ppermute(tokens, 'yz', pairs(1))  2.94 us
    ppermute x1, waiting for transfers between devices, on_device(): got = lax.ppermute(given, 'gx', swap)  1.27 us
    ppermute x1, waiting for transfers between devices, on_device(): other = lax.ppermute(sums, 'gx', swap)  1.16 us
  transfers between devices with their start and end apart: 6, of which 5 were waited for; matrix products, arithmetic and copies ran while one was open for 0% of the time, Pallas kernels for 1%

profile of v3, /device:TPU:0, one launch (start us, length us, event | category | flops | bytes accessed | tf_op | source)
XLA Modules:
  0.0 55.9 jit_solution(13893768463803425668)
XLA Ops:
  0.0 2.9 %collective-permute-start = (bf16[2,9216]{1,0:T(2,128)(2,1)}, bf16[2,9216]{1,0:T(2,128)(2,1)S(1)}, u32[]{:S(2)}, u32[]{:S(2)}) collective-permute-start(bf16[2,9216]{1,0:T(2,128)(2,1)} %tokens_hbm.1), channel_id=1, source_target_pairs={{0,1},{1,0},{2,3},{3,2},{4,5},{5,4},{6,7},{7,6},{8,9},{9,8},{10,11... | collective-permute-start | bytes 110600 | tf_op jit(solution)/shard_map/ppermute | solution.py:196
  3.6 0.8 %shard_map.64 = (bf16[2,9216]{1,0:T(2,128)(2,1)S(1)}, f32[1,9216]{1,0:T(1,128)S(1)}, s32[8,128]{1,0:T(8,128)S(1)}, bf16[28800,1024]{1,0:T(8,128)(2,1)}) custom-call(s32[1]{0:T(128)S(6)} %copy.7.lengths_ref, bf16[2,9216]{1,0:T(2,128)(2,1)} %tokens_hbm.1, f32[1,9216]{1,0:T(1,128)} %bitcast.5), custom_call_target="tpu_custom_call" | custom-call | flops 18432 | bytes 36864 | tf_op jit(solution)/shard_map/pallas_call | solution.py:34
  4.4 0.7 %collective-permute-done.rows_refs_1_ = bf16[2,9216]{1,0:T(2,128)(2,1)S(1)} collective-permute-done((bf16[2,9216]{1,0:T(2,128)(2,1)}, bf16[2,9216]{1,0:T(2,128)(2,1)S(1)}, u32[]{:S(2)}, u32[]{:S(2)}) %collective-permute-start) | collective-permute-done | bytes 36896 | tf_op jit(solution)/shard_map/ppermute | solution.py:196
  5.1 0.2 shard_map.65.sums_ref
  5.3 0.0 collective-permute-start.1
  5.3 1.2 %collective-permute-done.1.other_ref = f32[2,2,2,128]{3,2,1,0:T(2,128)S(1)} collective-permute-done((f32[2,2,2,128]{3,2,1,0:T(2,128)S(1)}, f32[2,2,2,128]{3,2,1,0:T(2,128)S(1)}, u32[]{:S(2)}, u32[]{:S(2)}) %collective-permute-start.1) | collective-permute-done | bytes 4128 | tf_op jit(solution)/shard_map/ppermute | solution.py:206
  6.5 0.0 copy-start
  6.5 0.2 shard_map.66.block_refs_0_
  6.7 0.0 copy-start.1
  6.7 4.2 %collective-permute-start.4 = (bf16[2,2,9216]{2,1,0:T(2,128)(2,1)S(1)}, bf16[2,2,9216]{2,1,0:T(2,128)(2,1)S(1)}, u32[]{:S(2)}, u32[]{:S(2)}) collective-permute-start(bf16[2,2,9216]{2,1,0:T(2,128)(2,1)S(1)} %shard_map.66.block_refs_0_), channel_id=1, source_target_pairs={{0,6},{1,7},{2,4},{3,5},{4,2},{5,3},{6,0},{7,1},{8,14},{9,15},{10,... | collective-permute-start | bytes 221192 | tf_op jit(solution)/shard_map/ppermute | solution.py:220
  10.9 0.0 collective-permute-start.3
  10.9 0.6 %collective-permute-start.2 = (bf16[2,2,9216]{2,1,0:T(2,128)(2,1)S(1)}, bf16[2,2,9216]{2,1,0:T(2,128)(2,1)S(1)}, u32[]{:S(2)}, u32[]{:S(2)}) collective-permute-start(bf16[2,2,9216]{2,1,0:T(2,128)(2,1)S(1)} %shard_map.66.block_refs_0_), channel_id=1, source_target_pairs={{0,2},{1,3},{2,0},{3,1},{4,6},{5,7},{6,4},{7,5},{8,10},{9,11},{10,... | collective-permute-start | bytes 221192 | tf_op jit(solution)/shard_map/ppermute | solution.py:220
  11.5 2.4 %collective-permute-done.4.block_refs_3_ = bf16[2,2,9216]{2,1,0:T(2,128)(2,1)S(1)} collective-permute-done((bf16[2,2,9216]{2,1,0:T(2,128)(2,1)S(1)}, bf16[2,2,9216]{2,1,0:T(2,128)(2,1)S(1)}, u32[]{:S(2)}, u32[]{:S(2)}) %collective-permute-start.4) | collective-permute-done | bytes 73760 | tf_op jit(solution)/shard_map/ppermute | solution.py:220
  13.9 3.5 %collective-permute-done.3.block_refs_2_ = bf16[2,2,9216]{2,1,0:T(2,128)(2,1)S(1)} collective-permute-done((bf16[2,2,9216]{2,1,0:T(2,128)(2,1)S(1)}, bf16[2,2,9216]{2,1,0:T(2,128)(2,1)S(1)}, u32[]{:S(2)}, u32[]{:S(2)}) %collective-permute-start.3) | collective-permute-done | bytes 73760 | tf_op jit(solution)/shard_map/ppermute | solution.py:220
  17.4 0.0 collective-permute-done.2.block_refs_1_
  17.4 0.0 copy-done
  17.4 0.0 slice-start
  17.4 7.8 %shard_map.67 = f32[16,1,1600]{2,1,0:T(1,128)S(1)} custom-call(bf16[2,2,9216]{2,1,0:T(2,128)(2,1)S(1)} %shard_map.66.block_refs_0_, bf16[2,2,9216]{2,1,0:T(2,128)(2,1)S(1)} %collective-permute-done.2.block_refs_1_, bf16[2,2,9216]{2,1,0:T(2,128)(2,1)S(1)} %collective-permute-done.3.block_refs_2_, ...), custom_call_target="tpu_custom_call" | custom-call | flops 471859200 | bytes 29491200 | tf_op jit(solution)/shard_map/pallas_call | solution.py:34
  25.2 12.3 %all_to_all.10.parts_ref = f32[16,1,1600]{2,1,0:T(1,128)S(1)} all-to-all(f32[16,1,1600]{2,1,0:T(1,128)S(1)} %shard_map.67), channel_id=1, replica_groups=mesh['ga'=2,'gx'=2,'yz'=8] {'yz','gx'}, dimensions={0} | all-to-all | bytes 204800 | tf_op jit(solution)/shard_map/all_to_all | solution.py:234
  37.5 0.0 copy-done.1
  37.5 0.0 slice-start.1
  37.5 0.0 slice-start.2
  37.5 0.0 slice-start.3
  37.5 0.0 slice-start.4
  37.5 0.0 slice-start.5
  37.5 0.0 slice-start.6
  37.5 0.5 shard_map.68
  38.0 12.1 %all_to_all.11.attended_ref = bf16[16,24,256]{2,1,0:T(8,128)(2,1)S(1)} all-to-all(bf16[16,24,256]{2,1,0:T(8,128)(2,1)S(1)} %shard_map.68), channel_id=1, replica_groups=mesh['ga'=2,'gx'=2,'yz'=8] {'yz','gx'}, dimensions={0} | all-to-all | bytes 393216 | tf_op jit(solution)/shard_map/all_to_all | solution.py:247
  50.2 0.0 slice-done
  50.2 0.0 slice-done.1
  50.2 0.0 slice-done.2
  50.2 0.0 slice-done.3
  50.2 0.0 slice-done.4
  50.2 0.0 slice-done.5
  50.2 0.0 slice-done.6
  50.2 3.8 %shard_map.69 = (f32[8,2304]{1,0:T(8,128)S(1)}, f32[8,2304]{1,0:T(8,128)S(1)}) custom-call(bf16[16,24,256]{2,1,0:T(8,128)(2,1)S(1)} %all_to_all.11.attended_ref, bf16[6144,2304]{1,0:T(8,128)(2,1)S(1)} %bitcast.4), custom_call_target="tpu_custom_call" | custom-call | flops 452984832 | bytes 28311552 | tf_op jit(solution)/shard_map/pallas_call | solution.py:34
  54.0 0.0 collective-permute-start.5
  54.0 1.3 %collective-permute-done.5 = f32[8,2304]{1,0:T(8,128)S(1)} collective-permute-done((f32[8,2304]{1,0:T(8,128)S(1)}, f32[8,2304]{1,0:T(8,128)S(1)}, u32[]{:S(2)}, u32[]{:S(2)}) %collective-permute-start.5) | collective-permute-done | bytes 73760 | tf_op jit(solution)/shard_map/ppermute | solution.py:262
  55.3 0.6 %add_convert_fusion = bf16[8,2304]{1,0:T(8,128)(2,1)} fusion(f32[8,2304]{1,0:T(8,128)S(1)} %get-tuple-element.15, f32[8,2304]{1,0:T(8,128)S(1)} %collective-permute-done.5), kind=kLoop, calls=%fused_computation | loop fusion | flops 36864 | bytes 184320 | tf_op jit(solution)/shard_map/convert_element_type | solution.py:263
  (1 shorter events, 0.0 us)
Async XLA Ops:
  0.0 5.1 %collective-permute-start = (bf16[2,9216]{1,0:T(2,128)(2,1)}, bf16[2,9216]{1,0:T(2,128)(2,1)S(1)}, u32[]{:S(2)}, u32[]{:S(2)}) collective-permute-start(bf16[2,9216]{1,0:T(2,128)(2,1)} %tokens_hbm.1), channel_id=1, source_target_pairs={{0,1},{1,0},{2,3},{3,2},{4,5},{5,4},{6,7},{7,6},{8,9},{9,8},{10,11... | collective-permute-start | bytes 110600 | tf_op jit(solution)/shard_map/ppermute | solution.py:196
  5.3 1.2 %collective-permute-start.1 = (f32[2,2,2,128]{3,2,1,0:T(2,128)S(1)}, f32[2,2,2,128]{3,2,1,0:T(2,128)S(1)}, u32[]{:S(2)}, u32[]{:S(2)}) collective-permute-start(f32[2,2,2,128]{3,2,1,0:T(2,128)S(1)} %shard_map.65.sums_ref), channel_id=1, source_target_pairs={{0,8},{8,0},{1,9},{9,1},{2,10},{10,2},{3,11},{11,3},{4,12},{12,4},... | collective-permute-start | bytes 12296 | tf_op jit(solution)/shard_map/ppermute | solution.py:206
  6.5 10.9 %copy-start = (bf16[9216,1600]{0,1:T(8,128)(2,1)S(1)}, bf16[9216,1600]{0,1:T(8,128)(2,1)}, u32[]{:S(2)}) copy-start(bf16[9216,1600]{0,1:T(8,128)(2,1)} %param.8) | copy-start | bytes 88473600
  6.7 30.8 %copy-start.1 = (bf16[1,512,512]{2,1,0:T(8,128)(2,1)S(1)}, bf16[1,512,512]{2,1,0:T(8,128)(2,1)}, u32[]{:S(2)}) copy-start(bf16[1,512,512]{2,1,0:T(8,128)(2,1)} %cache_ref.1) | copy-start | bytes 1572868
  6.7 7.2 %collective-permute-start.4 = (bf16[2,2,9216]{2,1,0:T(2,128)(2,1)S(1)}, bf16[2,2,9216]{2,1,0:T(2,128)(2,1)S(1)}, u32[]{:S(2)}, u32[]{:S(2)}) collective-permute-start(bf16[2,2,9216]{2,1,0:T(2,128)(2,1)S(1)} %shard_map.66.block_refs_0_), channel_id=1, source_target_pairs={{0,6},{1,7},{2,4},{3,5},{4,2},{5,3},{6,0},{7,1},{8,14},{9,15},{10,... | collective-permute-start | bytes 221192 | tf_op jit(solution)/shard_map/ppermute | solution.py:220
  10.9 6.5 %collective-permute-start.3 = (bf16[2,2,9216]{2,1,0:T(2,128)(2,1)S(1)}, bf16[2,2,9216]{2,1,0:T(2,128)(2,1)S(1)}, u32[]{:S(2)}, u32[]{:S(2)}) collective-permute-start(bf16[2,2,9216]{2,1,0:T(2,128)(2,1)S(1)} %shard_map.66.block_refs_0_), channel_id=1, source_target_pairs={{0,4},{1,5},{2,6},{3,7},{4,0},{5,1},{6,2},{7,3},{8,12},{9,13},{10,... | collective-permute-start | bytes 221192 | tf_op jit(solution)/shard_map/ppermute | solution.py:220
  10.9 6.5 %collective-permute-start.2 = (bf16[2,2,9216]{2,1,0:T(2,128)(2,1)S(1)}, bf16[2,2,9216]{2,1,0:T(2,128)(2,1)S(1)}, u32[]{:S(2)}, u32[]{:S(2)}) collective-permute-start(bf16[2,2,9216]{2,1,0:T(2,128)(2,1)S(1)} %shard_map.66.block_refs_0_), channel_id=1, source_target_pairs={{0,2},{1,3},{2,0},{3,1},{4,6},{5,7},{6,4},{7,5},{8,10},{9,11},{10,... | collective-permute-start | bytes 221192 | tf_op jit(solution)/shard_map/ppermute | solution.py:220
  17.4 32.8 %slice-start = ((s8[28311552]{0:T(1024)(128)(4,1)}), s8[3145728]{0:T(1024)(128)(4,1)S(1)}, s32[]{:S(2)}) async-start(s8[28311552]{0:T(1024)(128)(4,1)} %bitcast.3), calls=%async_computation.2 | async-start | bytes 6291456
  37.5 12.7 %slice-start.1 = ((s8[28311552]{0:T(1024)(128)(4,1)}), s8[4194304]{0:T(1024)(128)(4,1)S(1)}, s32[]{:S(2)}) async-start(s8[28311552]{0:T(1024)(128)(4,1)} %bitcast.3), calls=%async_computation.3 | async-start | bytes 8388608
  37.5 12.7 %slice-start.2 = ((s8[28311552]{0:T(1024)(128)(4,1)}), s8[4194304]{0:T(1024)(128)(4,1)S(1)}, s32[]{:S(2)}) async-start(s8[28311552]{0:T(1024)(128)(4,1)} %bitcast.3), calls=%async_computation.4 | async-start | bytes 8388608
  37.5 12.7 %slice-start.3 = ((s8[28311552]{0:T(1024)(128)(4,1)}), s8[4194304]{0:T(1024)(128)(4,1)S(1)}, s32[]{:S(2)}) async-start(s8[28311552]{0:T(1024)(128)(4,1)} %bitcast.3), calls=%async_computation.5 | async-start | bytes 8388608
  37.5 12.7 %slice-start.4 = ((s8[28311552]{0:T(1024)(128)(4,1)}), s8[4194304]{0:T(1024)(128)(4,1)S(1)}, s32[]{:S(2)}) async-start(s8[28311552]{0:T(1024)(128)(4,1)} %bitcast.3), calls=%async_computation.6 | async-start | bytes 8388608
  37.5 12.7 %slice-start.5 = ((s8[28311552]{0:T(1024)(128)(4,1)}), s8[4194304]{0:T(1024)(128)(4,1)S(1)}, s32[]{:S(2)}) async-start(s8[28311552]{0:T(1024)(128)(4,1)} %bitcast.3), calls=%async_computation.7 | async-start | bytes 8388608
  37.5 12.7 %slice-start.6 = ((s8[28311552]{0:T(1024)(128)(4,1)}), s8[4194304]{0:T(1024)(128)(4,1)S(1)}, s32[]{:S(2)}) async-start(s8[28311552]{0:T(1024)(128)(4,1)} %bitcast.3), calls=%async_computation.8 | async-start | bytes 8388608
  54.0 1.3 %collective-permute-start.5 = (f32[8,2304]{1,0:T(8,128)S(1)}, f32[8,2304]{1,0:T(8,128)S(1)}, u32[]{:S(2)}, u32[]{:S(2)}) collective-permute-start(f32[8,2304]{1,0:T(8,128)S(1)} %get-tuple-element.16), channel_id=1, source_target_pairs={{0,8},{8,0},{1,9},{9,1},{2,10},{10,2},{3,11},{11,3},{4,12},{12,4},... | collective-permute-start | bytes 221192 | tf_op jit(solution)/shard_map/ppermute | solution.py:262

commit v4 on v3

--- a/solution.py
+++ b/solution.py
@@ -10,6 +10,7 @@
 D = 18432
 HQ = 48
 HD = 256
+BLOCK = 256
 MIB = 1 << 20
 VMEM = pl.BlockSpec(memory_space=pltpu.VMEM)
 SMEM = pl.BlockSpec(memory_space=pltpu.SMEM)
@@ -75,7 +76,13 @@
         out_ref[i] = normed
 
 
-def project_kernel(order, block_refs, weight_ref, out_ref, wide):
+def dot_last(left, right):
+    return lax.dot_general(
+        left, right, (((1,), (1,)), ((), ())), preferred_element_type=jnp.float32
+    )
+
+
+def project_kernel(order, block_refs, weight_ref, out_ref, wide, rows, terms):
     group = lax.axis_index("yz")
     at, places = 0, []
     for ref, origins in zip(block_refs, order):
@@ -84,10 +91,23 @@
             wide[at : at + per, :] = ref[i].astype(jnp.float32)
             places.extend(origin(group) * per + r for r in range(per))
             at += per
-    rows = wide[...].astype(jnp.bfloat16)
-    terms = lax.dot_general(
-        rows, weight_ref[...], (((1,), (1,)), ((), ())), preferred_element_type=jnp.float32
-    )
+    rows[...] = wide[...].astype(jnp.bfloat16)
+    batch, depth = rows.shape
+    width = weight_ref.shape[0]
+    at = 0
+    while width - at >= 2 * BLOCK:
+        middle, end = at + BLOCK, at + 2 * BLOCK
+        first = jnp.zeros((batch, BLOCK), jnp.float32)
+        second = jnp.zeros((BLOCK, batch), jnp.float32)
+        for k in range(0, depth, BLOCK):
+            some = rows[:, k : k + BLOCK]
+            second = second + dot_last(weight_ref[middle:end, k : k + BLOCK], some)
+            first = first + dot_last(some, weight_ref[at:middle, k : k + BLOCK])
+        terms[:, at:middle] = first
+        terms[:, middle:end] = second.T
+        at = end
+    if at < width:
+        terms[:, at:] = dot_last(rows[...], weight_ref[at:, :])
     for i, place in enumerate(places):
         out_ref[place] = terms[i : i + 1, :]
 
@@ -225,8 +245,12 @@
             functools.partial(project_kernel, order),
             jax.ShapeDtypeStruct((members, 1, width), f32),
             [[VMEM] * len(blocks), VMEM],
-            [pltpu.VMEM((batch, depth), f32)],
-            bytes_of(((batch, depth), 8), ((batch, width + 128), 16)),
+            [
+                pltpu.VMEM((batch, depth), f32),
+                pltpu.VMEM((batch, depth), bf16),
+                pltpu.VMEM((batch, width), f32),
+            ],
+            bytes_of(((batch, depth), 8), ((batch, width + 128), 16), ((BLOCK, BLOCK), 8)),
             (2 * batch * depth * width, depth * width * 2),
             blocks,
             w_in,

time: 56.1 us -> 52.8 us (0.941)
  Pallas kernels: 13.3 us -> 9.99 us
    pallas_call x6, Pallas kernels: 13.3 us -> 9.99 us  [call(): pl.pallas_call(kernel, out_shape=outs, in_specs=in_specs, out_specs=jax.t...]
  transfers between devices with their start and end apart: 6 -> 6, of which waited for: 5 -> 5; matrix products, arithmetic and copies ran while one was open for 0% -> 0% of each run, Pallas kernels for 1% -> 2%
where the time goes in v4:
time: 52.8 us; the launch traced here: 52.6 us
  blocking collectives  24.4 us (46%)
  Pallas kernels  9.99 us (19%)
  waiting for transfers between devices  8.98 us (17%)
  starting transfers between devices  7.78 us (15%)
  between operations  0.77 us (1%)
  other arithmetic  0.63 us (1%)
    all_to_all x1, blocking collectives, on_device(): moved = lax.all_to_all(parts, ('yz', 'gx'), 0, 0, tiled=True)  12.3 us
    all_to_all x1, blocking collectives, on_device(): gathered = lax.all_to_all(attended, ('yz', 'gx'), 0, 0, tiled=True)  12.1 us
    pallas_call x6, Pallas kernels, call(): pl.pallas_call(kernel, out_shape=outs, in_specs=in_specs, out_specs=jax.t...  9.99 us
    ppermute x3, waiting for transfers between devices, on_device(): lax.ppermute(normed, 'yz', pairs(k))  5.86 us
    ppermute x3, starting transfers between devices, on_device(): lax.ppermute(normed, 'yz', pairs(k))  4.84 us
    ppermute x1, starting transfers between devices, on_device(): mate = lax.ppermute(tokens, 'yz', pairs(1))  2.94 us
    ppermute x1, waiting for transfers between devices, on_device(): got = lax.ppermute(given, 'gx', swap)  1.27 us
    ppermute x1, waiting for transfers between devices, on_device(): other = lax.ppermute(sums, 'gx', swap)  1.16 us
  transfers between devices with their start and end apart: 6, of which 5 were waited for; matrix products, arithmetic and copies ran while one was open for 0% of the time, Pallas kernels for 2%

profile of v4, /device:TPU:0, one launch (start us, length us, event | category | flops | bytes accessed | tf_op | source)
XLA Modules:
  0.0 52.6 jit_solution(3480083192845229314)
XLA Ops:
  0.0 2.9 %collective-permute-start = (bf16[2,9216]{1,0:T(2,128)(2,1)}, bf16[2,9216]{1,0:T(2,128)(2,1)S(1)}, u32[]{:S(2)}, u32[]{:S(2)}) collective-permute-start(bf16[2,9216]{1,0:T(2,128)(2,1)} %tokens_hbm.1), channel_id=1, source_target_pairs={{0,1},{1,0},{2,3},{3,2},{4,5},{5,4},{6,7},{7,6},{8,9},{9,8},{10,11... | collective-permute-start | bytes 110600 | tf_op jit(solution)/shard_map/ppermute | solution.py:216
  3.6 0.8 %shard_map.64 = (bf16[2,9216]{1,0:T(2,128)(2,1)S(1)}, f32[1,9216]{1,0:T(1,128)S(1)}, s32[8,128]{1,0:T(8,128)S(1)}, bf16[28800,1024]{1,0:T(8,128)(2,1)}) custom-call(s32[1]{0:T(128)S(6)} %copy.7.lengths_ref, bf16[2,9216]{1,0:T(2,128)(2,1)} %tokens_hbm.1, f32[1,9216]{1,0:T(1,128)} %bitcast.5), custom_call_target="tpu_custom_call" | custom-call | flops 18432 | bytes 36864 | tf_op jit(solution)/shard_map/pallas_call | solution.py:35
  4.4 0.7 %collective-permute-done.rows_refs_1_ = bf16[2,9216]{1,0:T(2,128)(2,1)S(1)} collective-permute-done((bf16[2,9216]{1,0:T(2,128)(2,1)}, bf16[2,9216]{1,0:T(2,128)(2,1)S(1)}, u32[]{:S(2)}, u32[]{:S(2)}) %collective-permute-start) | collective-permute-done | bytes 36896 | tf_op jit(solution)/shard_map/ppermute | solution.py:216
  5.1 0.2 shard_map.65.sums_ref
  5.3 0.0 collective-permute-start.1
  5.3 1.2 %collective-permute-done.1.other_ref = f32[2,2,2,128]{3,2,1,0:T(2,128)S(1)} collective-permute-done((f32[2,2,2,128]{3,2,1,0:T(2,128)S(1)}, f32[2,2,2,128]{3,2,1,0:T(2,128)S(1)}, u32[]{:S(2)}, u32[]{:S(2)}) %collective-permute-start.1) | collective-permute-done | bytes 4128 | tf_op jit(solution)/shard_map/ppermute | solution.py:226
  6.5 0.0 copy-start
  6.5 0.1 shard_map.66.block_refs_0_
  6.7 0.0 copy-start.1
  6.7 4.2 %collective-permute-start.4 = (bf16[2,2,9216]{2,1,0:T(2,128)(2,1)S(1)}, bf16[2,2,9216]{2,1,0:T(2,128)(2,1)S(1)}, u32[]{:S(2)}, u32[]{:S(2)}) collective-permute-start(bf16[2,2,9216]{2,1,0:T(2,128)(2,1)S(1)} %shard_map.66.block_refs_0_), channel_id=1, source_target_pairs={{0,6},{1,7},{2,4},{3,5},{4,2},{5,3},{6,0},{7,1},{8,14},{9,15},{10,... | collective-permute-start | bytes 221192 | tf_op jit(solution)/shard_map/ppermute | solution.py:240
  10.9 0.0 collective-permute-start.3
  10.9 0.6 %collective-permute-start.2 = (bf16[2,2,9216]{2,1,0:T(2,128)(2,1)S(1)}, bf16[2,2,9216]{2,1,0:T(2,128)(2,1)S(1)}, u32[]{:S(2)}, u32[]{:S(2)}) collective-permute-start(bf16[2,2,9216]{2,1,0:T(2,128)(2,1)S(1)} %shard_map.66.block_refs_0_), channel_id=1, source_target_pairs={{0,2},{1,3},{2,0},{3,1},{4,6},{5,7},{6,4},{7,5},{8,10},{9,11},{10,... | collective-permute-start | bytes 221192 | tf_op jit(solution)/shard_map/ppermute | solution.py:240
  11.5 2.4 %collective-permute-done.4.block_refs_3_ = bf16[2,2,9216]{2,1,0:T(2,128)(2,1)S(1)} collective-permute-done((bf16[2,2,9216]{2,1,0:T(2,128)(2,1)S(1)}, bf16[2,2,9216]{2,1,0:T(2,128)(2,1)S(1)}, u32[]{:S(2)}, u32[]{:S(2)}) %collective-permute-start.4) | collective-permute-done | bytes 73760 | tf_op jit(solution)/shard_map/ppermute | solution.py:240
  13.9 3.5 %collective-permute-done.3.block_refs_2_ = bf16[2,2,9216]{2,1,0:T(2,128)(2,1)S(1)} collective-permute-done((bf16[2,2,9216]{2,1,0:T(2,128)(2,1)S(1)}, bf16[2,2,9216]{2,1,0:T(2,128)(2,1)S(1)}, u32[]{:S(2)}, u32[]{:S(2)}) %collective-permute-start.3) | collective-permute-done | bytes 73760 | tf_op jit(solution)/shard_map/ppermute | solution.py:240
  17.4 0.0 collective-permute-done.2.block_refs_1_
  17.4 0.0 copy-done
  17.4 0.0 slice-start
  17.4 4.5 %shard_map.67 = f32[16,1,1600]{2,1,0:T(1,128)S(1)} custom-call(bf16[2,2,9216]{2,1,0:T(2,128)(2,1)S(1)} %shard_map.66.block_refs_0_, bf16[2,2,9216]{2,1,0:T(2,128)(2,1)S(1)} %collective-permute-done.2.block_refs_1_, bf16[2,2,9216]{2,1,0:T(2,128)(2,1)S(1)} %collective-permute-done.3.block_refs_2_, ...), custom_call_target="tpu_custom_call" | custom-call | flops 471859200 | bytes 29491200 | tf_op jit(solution)/shard_map/pallas_call | solution.py:35
  21.9 12.3 %all_to_all.10.parts_ref = f32[16,1,1600]{2,1,0:T(1,128)S(1)} all-to-all(f32[16,1,1600]{2,1,0:T(1,128)S(1)} %shard_map.67), channel_id=1, replica_groups=mesh['ga'=2,'gx'=2,'yz'=8] {'yz','gx'}, dimensions={0} | all-to-all | bytes 204800 | tf_op jit(solution)/shard_map/all_to_all | solution.py:258
  34.2 0.0 copy-done.1
  34.2 0.0 slice-start.1
  34.2 0.0 slice-start.2
  34.2 0.0 slice-start.3
  34.2 0.0 slice-start.4
  34.2 0.0 slice-start.5
  34.2 0.0 slice-start.6
  34.2 0.5 shard_map.68
  34.7 12.1 %all_to_all.11.attended_ref = bf16[16,24,256]{2,1,0:T(8,128)(2,1)S(1)} all-to-all(bf16[16,24,256]{2,1,0:T(8,128)(2,1)S(1)} %shard_map.68), channel_id=1, replica_groups=mesh['ga'=2,'gx'=2,'yz'=8] {'yz','gx'}, dimensions={0} | all-to-all | bytes 393216 | tf_op jit(solution)/shard_map/all_to_all | solution.py:271
  46.9 0.0 slice-done
  46.9 0.0 slice-done.1
  46.9 0.0 slice-done.2
  46.9 0.0 slice-done.3
  46.9 0.0 slice-done.4
  46.9 0.0 slice-done.5
  46.9 0.0 slice-done.6
  46.9 3.8 %shard_map.69 = (f32[8,2304]{1,0:T(8,128)S(1)}, f32[8,2304]{1,0:T(8,128)S(1)}) custom-call(bf16[16,24,256]{2,1,0:T(8,128)(2,1)S(1)} %all_to_all.11.attended_ref, bf16[6144,2304]{1,0:T(8,128)(2,1)S(1)} %bitcast.4), custom_call_target="tpu_custom_call" | custom-call | flops 452984832 | bytes 28311552 | tf_op jit(solution)/shard_map/pallas_call | solution.py:35
  50.7 0.0 collective-permute-start.5
  50.7 1.3 %collective-permute-done.5 = f32[8,2304]{1,0:T(8,128)S(1)} collective-permute-done((f32[8,2304]{1,0:T(8,128)S(1)}, f32[8,2304]{1,0:T(8,128)S(1)}, u32[]{:S(2)}, u32[]{:S(2)}) %collective-permute-start.5) | collective-permute-done | bytes 73760 | tf_op jit(solution)/shard_map/ppermute | solution.py:286
  52.0 0.6 %add_convert_fusion = bf16[8,2304]{1,0:T(8,128)(2,1)} fusion(f32[8,2304]{1,0:T(8,128)S(1)} %get-tuple-element.15, f32[8,2304]{1,0:T(8,128)S(1)} %collective-permute-done.5), kind=kLoop, calls=%fused_computation | loop fusion | flops 36864 | bytes 184320 | tf_op jit(solution)/shard_map/convert_element_type | solution.py:287
  (1 shorter events, 0.0 us)
Async XLA Ops:
  0.0 5.1 %collective-permute-start = (bf16[2,9216]{1,0:T(2,128)(2,1)}, bf16[2,9216]{1,0:T(2,128)(2,1)S(1)}, u32[]{:S(2)}, u32[]{:S(2)}) collective-permute-start(bf16[2,9216]{1,0:T(2,128)(2,1)} %tokens_hbm.1), channel_id=1, source_target_pairs={{0,1},{1,0},{2,3},{3,2},{4,5},{5,4},{6,7},{7,6},{8,9},{9,8},{10,11... | collective-permute-start | bytes 110600 | tf_op jit(solution)/shard_map/ppermute | solution.py:216
  5.3 1.2 %collective-permute-start.1 = (f32[2,2,2,128]{3,2,1,0:T(2,128)S(1)}, f32[2,2,2,128]{3,2,1,0:T(2,128)S(1)}, u32[]{:S(2)}, u32[]{:S(2)}) collective-permute-start(f32[2,2,2,128]{3,2,1,0:T(2,128)S(1)} %shard_map.65.sums_ref), channel_id=1, source_target_pairs={{0,8},{8,0},{1,9},{9,1},{2,10},{10,2},{3,11},{11,3},{4,12},{12,4},... | collective-permute-start | bytes 12296 | tf_op jit(solution)/shard_map/ppermute | solution.py:226
  6.5 10.9 %copy-start = (bf16[9216,1600]{0,1:T(8,128)(2,1)S(1)}, bf16[9216,1600]{0,1:T(8,128)(2,1)}, u32[]{:S(2)}) copy-start(bf16[9216,1600]{0,1:T(8,128)(2,1)} %param.8) | copy-start | bytes 88473600
  6.7 27.5 %copy-start.1 = (bf16[1,512,512]{2,1,0:T(8,128)(2,1)S(1)}, bf16[1,512,512]{2,1,0:T(8,128)(2,1)}, u32[]{:S(2)}) copy-start(bf16[1,512,512]{2,1,0:T(8,128)(2,1)} %cache_ref.1) | copy-start | bytes 1572868
  6.7 7.2 %collective-permute-start.4 = (bf16[2,2,9216]{2,1,0:T(2,128)(2,1)S(1)}, bf16[2,2,9216]{2,1,0:T(2,128)(2,1)S(1)}, u32[]{:S(2)}, u32[]{:S(2)}) collective-permute-start(bf16[2,2,9216]{2,1,0:T(2,128)(2,1)S(1)} %shard_map.66.block_refs_0_), channel_id=1, source_target_pairs={{0,6},{1,7},{2,4},{3,5},{4,2},{5,3},{6,0},{7,1},{8,14},{9,15},{10,... | collective-permute-start | bytes 221192 | tf_op jit(solution)/shard_map/ppermute | solution.py:240
  10.9 6.5 %collective-permute-start.3 = (bf16[2,2,9216]{2,1,0:T(2,128)(2,1)S(1)}, bf16[2,2,9216]{2,1,0:T(2,128)(2,1)S(1)}, u32[]{:S(2)}, u32[]{:S(2)}) collective-permute-start(bf16[2,2,9216]{2,1,0:T(2,128)(2,1)S(1)} %shard_map.66.block_refs_0_), channel_id=1, source_target_pairs={{0,4},{1,5},{2,6},{3,7},{4,0},{5,1},{6,2},{7,3},{8,12},{9,13},{10,... | collective-permute-start | bytes 221192 | tf_op jit(solution)/shard_map/ppermute | solution.py:240
  10.9 6.5 %collective-permute-start.2 = (bf16[2,2,9216]{2,1,0:T(2,128)(2,1)S(1)}, bf16[2,2,9216]{2,1,0:T(2,128)(2,1)S(1)}, u32[]{:S(2)}, u32[]{:S(2)}) collective-permute-start(bf16[2,2,9216]{2,1,0:T(2,128)(2,1)S(1)} %shard_map.66.block_refs_0_), channel_id=1, source_target_pairs={{0,2},{1,3},{2,0},{3,1},{4,6},{5,7},{6,4},{7,5},{8,10},{9,11},{10,... | collective-permute-start | bytes 221192 | tf_op jit(solution)/shard_map/ppermute | solution.py:240
  17.4 29.5 %slice-start = ((s8[28311552]{0:T(1024)(128)(4,1)}), s8[3145728]{0:T(1024)(128)(4,1)S(1)}, s32[]{:S(2)}) async-start(s8[28311552]{0:T(1024)(128)(4,1)} %bitcast.3), calls=%async_computation.2 | async-start | bytes 6291456
  34.2 12.7 %slice-start.1 = ((s8[28311552]{0:T(1024)(128)(4,1)}), s8[4194304]{0:T(1024)(128)(4,1)S(1)}, s32[]{:S(2)}) async-start(s8[28311552]{0:T(1024)(128)(4,1)} %bitcast.3), calls=%async_computation.3 | async-start | bytes 8388608
  34.2 12.7 %slice-start.2 = ((s8[28311552]{0:T(1024)(128)(4,1)}), s8[4194304]{0:T(1024)(128)(4,1)S(1)}, s32[]{:S(2)}) async-start(s8[28311552]{0:T(1024)(128)(4,1)} %bitcast.3), calls=%async_computation.4 | async-start | bytes 8388608
  34.2 12.7 %slice-start.3 = ((s8[28311552]{0:T(1024)(128)(4,1)}), s8[4194304]{0:T(1024)(128)(4,1)S(1)}, s32[]{:S(2)}) async-start(s8[28311552]{0:T(1024)(128)(4,1)} %bitcast.3), calls=%async_computation.5 | async-start | bytes 8388608
  34.2 12.7 %slice-start.4 = ((s8[28311552]{0:T(1024)(128)(4,1)}), s8[4194304]{0:T(1024)(128)(4,1)S(1)}, s32[]{:S(2)}) async-start(s8[28311552]{0:T(1024)(128)(4,1)} %bitcast.3), calls=%async_computation.6 | async-start | bytes 8388608
  34.2 12.7 %slice-start.5 = ((s8[28311552]{0:T(1024)(128)(4,1)}), s8[4194304]{0:T(1024)(128)(4,1)S(1)}, s32[]{:S(2)}) async-start(s8[28311552]{0:T(1024)(128)(4,1)} %bitcast.3), calls=%async_computation.7 | async-start | bytes 8388608
  34.2 12.7 %slice-start.6 = ((s8[28311552]{0:T(1024)(128)(4,1)}), s8[4194304]{0:T(1024)(128)(4,1)S(1)}, s32[]{:S(2)}) async-start(s8[28311552]{0:T(1024)(128)(4,1)} %bitcast.3), calls=%async_computation.8 | async-start | bytes 8388608
  50.7 1.3 %collective-permute-start.5 = (f32[8,2304]{1,0:T(8,128)S(1)}, f32[8,2304]{1,0:T(8,128)S(1)}, u32[]{:S(2)}, u32[]{:S(2)}) collective-permute-start(f32[8,2304]{1,0:T(8,128)S(1)} %get-tuple-element.16), channel_id=1, source_target_pairs={{0,8},{8,0},{1,9},{9,1},{2,10},{10,2},{3,11},{11,3},{4,12},{12,4},... | collective-permute-start | bytes 221192 | tf_op jit(solution)/shard_map/ppermute | solution.py:286

commit v5 on v4

--- a/solution.py
+++ b/solution.py
@@ -57,23 +57,21 @@
         copy.wait()
 
 
-def sums_kernel(rows_refs, sums_ref):
+def column_kernel(rows_refs, spare_hbm, column_ref, sums_ref):
+    lanes = sums_ref.shape[2:]
     for i, ref in enumerate(rows_refs):
+        column_ref[i] = ref[...]
         rows = ref[...].astype(jnp.float32)
-        lanes = sums_ref.shape[2:]
         sums_ref[i, 0] = jnp.broadcast_to(jnp.sum(rows, axis=1, keepdims=True), lanes)
         sums_ref[i, 1] = jnp.broadcast_to(jnp.sum(rows * rows, axis=1, keepdims=True), lanes)
 
 
-def norm_kernel(rows_refs, gain_ref, sums_ref, other_ref, spare_hbm, out_ref):
-    for i, ref in enumerate(rows_refs):
-        total = sums_ref[i, 0][:, 0:1] + other_ref[i, 0][:, 0:1]
-        squares = sums_ref[i, 1][:, 0:1] + other_ref[i, 1][:, 0:1]
-        mean = total / D
-        var = squares / D - mean * mean
-        rows = ref[...].astype(jnp.float32)
-        normed = ((rows - mean) * lax.rsqrt(var + 1e-06) * gain_ref[...]).astype(jnp.bfloat16)
-        out_ref[i] = normed
+def stats_kernel(sums_ref, other_ref, stats_ref):
+    for i in range(sums_ref.shape[0]):
+        mean = (sums_ref[i, 0] + other_ref[i, 0]) / D
+        var = (sums_ref[i, 1] + other_ref[i, 1]) / D - mean * mean
+        stats_ref[i, 0] = mean
+        stats_ref[i, 1] = lax.rsqrt(var + 1e-06)
 
 
 def dot_last(left, right):
@@ -82,16 +80,21 @@
     )
 
 
-def project_kernel(order, block_refs, weight_ref, out_ref, wide, rows, terms):
+def project_kernel(
+    order, block_refs, stats_refs, gain_ref, weight_ref, out_ref, wide, stats, rows, terms
+):
     group = lax.axis_index("yz")
     at, places = 0, []
-    for ref, origins in zip(block_refs, order):
+    for ref, stats_ref, origins in zip(block_refs, stats_refs, order):
         per = ref.shape[1]
         for i, origin in enumerate(origins):
             wide[at : at + per, :] = ref[i].astype(jnp.float32)
+            stats[0, at : at + per, :] = stats_ref[i, 0]
+            stats[1, at : at + per, :] = stats_ref[i, 1]
             places.extend(origin(group) * per + r for r in range(per))
             at += per
-    rows[...] = wide[...].astype(jnp.bfloat16)
+    mean, scale = stats[0][:, 0:1], stats[1][:, 0:1]
+    rows[...] = ((wide[...] - mean) * scale * gain_ref[...]).astype(jnp.bfloat16)
     batch, depth = rows.shape
     width = weight_ref.shape[0]
     at = 0
@@ -202,7 +205,7 @@
                 jax.ShapeDtypeStruct((per, depth), bf16),
                 jax.ShapeDtypeStruct((1, depth), f32),
                 jax.ShapeDtypeStruct((8, 128), jnp.int32),
-                pltpu.HBM((2 * depth * width // 1024, 1024), bf16),
+                pltpu.HBM((5 * depth * width // 4096, 1024), bf16),
             ],
             [SMEM, ANY, ANY],
             [pltpu.SemaphoreType.DMA((2,))],
@@ -213,60 +216,68 @@
             pltpu.with_memory_space_constraint(gain.reshape(1, -1), pltpu.HBM),
         )
         spare = pltpu.with_memory_space_constraint(spare, pltpu.HBM)
-        mate = lax.ppermute(tokens, "yz", pairs(1))
-        sums = call(
-            sums_kernel,
-            jax.ShapeDtypeStruct((2, 2, per, 128), f32),
-            [[VMEM, VMEM]],
+        steps = range(0, groups, 2)
+        mates = [own] + [lax.ppermute(tokens, "yz", pairs(k)) for k in steps[1:]]
+        column, sums = call(
+            column_kernel,
+            [
+                jax.ShapeDtypeStruct((len(steps), per, depth), bf16),
+                jax.ShapeDtypeStruct((len(steps), 2, per, 128), f32),
+            ],
+            [[VMEM] * len(steps), ANY],
             [],
-            bytes_of(((8, depth), 8)),
-            (8 * per * depth, 4 * per * depth),
-            [own, mate],
-        )
+            bytes_of(((8, depth), 16)),
+            (4 * batch * depth, 4 * batch * depth),
+            mates,
+            spare,
+        )
+        beside = lax.ppermute(column, "yz", pairs(1))
         other = lax.ppermute(sums, "gx", swap)
-        normed = call(
-            norm_kernel,
-            jax.ShapeDtypeStruct((2, per, depth), bf16),
-            [[VMEM, VMEM], VMEM, VMEM, VMEM, ANY],
+        stats = call(
+            stats_kernel,
+            jax.ShapeDtypeStruct(sums.shape, f32),
+            [VMEM, VMEM],
             [],
-            bytes_of(((8, depth), 24)),
-            (12 * per * depth, 4 * per * depth),
-            [own, mate],
-            scale,
+            bytes_of(((16, 128), 16)),
+            (64 * 128, 64 * 128),
             sums,
             other,
-            spare,
-        )
-        blocks = [normed] + [lax.ppermute(normed, "yz", pairs(k)) for k in range(2, groups, 2)]
+        )
+        blocks = [column, beside]
+        scales = [stats, lax.ppermute(stats, "yz", pairs(1))]
         order = [
-            [lambda g, k=k: g ^ k, lambda g, k=k: g ^ k ^ 1] for k in range(0, groups, 2)
+            [lambda g, k=k: g ^ k for k in steps],
+            [lambda g, k=k: g ^ k ^ 1 for k in steps],
         ]
         parts = call(
             functools.partial(project_kernel, order),
             jax.ShapeDtypeStruct((members, 1, width), f32),
-            [[VMEM] * len(blocks), VMEM],
+            [[VMEM] * len(blocks), [VMEM] * len(blocks), VMEM, VMEM],
             [
                 pltpu.VMEM((batch, depth), f32),
+                pltpu.VMEM((2, batch, 128), f32),
                 pltpu.VMEM((batch, depth), bf16),
                 pltpu.VMEM((batch, width), f32),
             ],
-            bytes_of(((batch, depth), 8), ((batch, width + 128), 16), ((BLOCK, BLOCK), 8)),
+            bytes_of(((batch, depth), 12), ((batch, width + 128), 16), ((BLOCK, BLOCK), 8)),
             (2 * batch * depth * width, depth * width * 2),
             blocks,
+            scales,
+            scale,
             w_in,
         )
         moved = lax.all_to_all(parts, ("yz", "gx"), 0, 0, tiled=True)
         attended = call(
             functools.partial(attend_kernel, halves),
             jax.ShapeDtypeStruct((members, HQ // halves, HD), bf16),
-            [VMEM, VMEM, VMEM, [ANY] * 4],
+            [VMEM, VMEM, VMEM, [ANY] * 7],
             [pltpu.VMEM((HQ + 8, HD), f32)],
             bytes_of(((members, HQ // halves, HD), 4), ((512, 512), 4), ((members, 8, width + 128), 8)),
             (4 * HQ * 512 * HD, w_out.shape[0] * wide_out * 2),
             used,
             moved,
             kv_cache,
-            [spare] * 4,
+            [spare] * 7,
         )
         gathered = lax.all_to_all(attended, ("yz", "gx"), 0, 0, tiled=True)
         size = batch // halves

time: 52.8 us -> 51.4 us (0.973)
  blocking collectives: 24.4 us -> 22.3 us
  between operations: 0.77 us -> 1.52 us
  Pallas kernels: 9.99 us -> 10.6 us
  waiting for transfers between devices: 8.98 us -> 8.42 us
    all_to_all x1, blocking collectives: 12.3 us -> 10.2 us  [on_device(): moved = lax.all_to_all(parts, ('yz', 'gx'), 0, 0, tiled=True)]
    pallas_call x6, Pallas kernels: 9.99 us -> 10.6 us  [call(): pl.pallas_call(kernel, out_shape=outs, in_specs=in_specs, out_specs=jax.t...]
    ppermute x4 -> x5, waiting for transfers between devices: 6.54 us -> 5.98 us  [the longest x1 3.12 us: on_device(): scales = [stats, lax.ppermute(stats, 'yz', pairs(1))]]
    ppermute x4 -> x5, starting transfers between devices: 7.78 us -> 7.71 us  [the longest x3 5.62 us: on_device(): mates = [own] + [lax.ppermute(tokens, 'yz', pairs(k)) for k in steps[1:]]]
  transfers between devices with their start and end apart: 6 -> 7, of which waited for: 5 -> 5; matrix products, arithmetic and copies ran while one was open for 0% -> 0% of each run, Pallas kernels for 2% -> 2%
where the time goes in v5:
time: 51.4 us; the launch traced here: 51.2 us
  blocking collectives  22.3 us (43%)
  Pallas kernels  10.6 us (21%)
  waiting for transfers between devices  8.42 us (16%)
  starting transfers between devices  7.71 us (15%)
  between operations  1.52 us (3%)
  other arithmetic  0.63 us (1%)
    all_to_all x1, blocking collectives, on_device(): gathered = lax.all_to_all(attended, ('yz', 'gx'), 0, 0, tiled=True)  12.1 us
    pallas_call x6, Pallas kernels, call(): pl.pallas_call(kernel, out_shape=outs, in_specs=in_specs, out_specs=jax.t...  10.6 us
    all_to_all x1, blocking collectives, on_device(): moved = lax.all_to_all(parts, ('yz', 'gx'), 0, 0, tiled=True)  10.2 us
    ppermute x3, starting transfers between devices, on_device(): mates = [own] + [lax.ppermute(tokens, 'yz', pairs(k)) for k in steps[1:]]  5.62 us
    ppermute x1, waiting for transfers between devices, on_device(): scales = [stats, lax.ppermute(stats, 'yz', pairs(1))]  3.12 us
    ppermute x3, waiting for transfers between devices, on_device(): mates = [own] + [lax.ppermute(tokens, 'yz', pairs(k)) for k in steps[1:]]  2.86 us
    ppermute x1, starting transfers between devices, on_device(): beside = lax.ppermute(column, 'yz', pairs(1))  1.49 us
    ppermute x1, waiting for transfers between devices, on_device(): got = lax.ppermute(given, 'gx', swap)  1.27 us
  transfers between devices with their start and end apart: 7, of which 5 were waited for; matrix products, arithmetic and copies ran while one was open for 0% of the time, Pallas kernels for 2%

profile of v5, /device:TPU:0, one launch (start us, length us, event | category | flops | bytes accessed | tf_op | source)
XLA Modules:
  0.0 51.2 jit_solution(1636785583493235748)
XLA Ops:
  0.0 0.0 copy-start
  0.0 3.0 %collective-permute-start = (bf16[2,9216]{1,0:T(2,128)(2,1)}, bf16[2,9216]{1,0:T(2,128)(2,1)S(1)}, u32[]{:S(2)}, u32[]{:S(2)}) collective-permute-start(bf16[2,9216]{1,0:T(2,128)(2,1)} %tokens_hbm.1), channel_id=1, source_target_pairs={{0,2},{1,3},{2,0},{3,1},{4,6},{5,7},{6,4},{7,5},{8,10},{9,11},{10,... | collective-permute-start | bytes 110600 | tf_op jit(solution)/shard_map/ppermute | solution.py:220
  3.0 2.5 %collective-permute-start.2 = (bf16[2,9216]{1,0:T(2,128)(2,1)}, bf16[2,9216]{1,0:T(2,128)(2,1)S(1)}, u32[]{:S(2)}, u32[]{:S(2)}) collective-permute-start(bf16[2,9216]{1,0:T(2,128)(2,1)} %tokens_hbm.1), channel_id=1, source_target_pairs={{0,6},{1,7},{2,4},{3,5},{4,2},{5,3},{6,0},{7,1},{8,14},{9,15},{10,... | collective-permute-start | bytes 110600 | tf_op jit(solution)/shard_map/ppermute | solution.py:220
  5.5 0.1 collective-permute-start.1
  7.0 1.1 %shard_map.64 = (bf16[2,9216]{1,0:T(2,128)(2,1)S(1)}, f32[1,9216]{1,0:T(1,128)S(1)}, s32[8,128]{1,0:T(8,128)S(1)}, bf16[18000,1024]{1,0:T(8,128)(2,1)}) custom-call(s32[1]{0:T(128)S(6)} %copy.7.lengths_ref, bf16[2,9216]{1,0:T(2,128)(2,1)} %tokens_hbm.1, f32[1,9216]{1,0:T(1,128)} %bitcast.5), custom_call_target="tpu_custom_call" | custom-call | flops 18432 | bytes 36864 | tf_op jit(solution)/shard_map/pallas_call | solution.py:35
  8.1 0.0 collective-permute-done.rows_refs_1_
  8.1 1.4 %collective-permute-done.2.rows_refs_3_ = bf16[2,9216]{1,0:T(2,128)(2,1)S(1)} collective-permute-done((bf16[2,9216]{1,0:T(2,128)(2,1)}, bf16[2,9216]{1,0:T(2,128)(2,1)S(1)}, u32[]{:S(2)}, u32[]{:S(2)}) %collective-permute-start.2) | collective-permute-done | bytes 36896 | tf_op jit(solution)/shard_map/ppermute | solution.py:220
  9.5 1.5 %collective-permute-done.1.rows_refs_2_ = bf16[2,9216]{1,0:T(2,128)(2,1)S(1)} collective-permute-done((bf16[2,9216]{1,0:T(2,128)(2,1)}, bf16[2,9216]{1,0:T(2,128)(2,1)S(1)}, u32[]{:S(2)}, u32[]{:S(2)}) %collective-permute-start.1) | collective-permute-done | bytes 36896 | tf_op jit(solution)/shard_map/ppermute | solution.py:220
  11.0 0.0 copy-start.1
  11.0 0.4 shard_map.65
  11.3 1.5 %collective-permute-start.3 = (bf16[4,2,9216]{2,1,0:T(2,128)(2,1)S(1)}, bf16[4,2,9216]{2,1,0:T(2,128)(2,1)S(1)}, u32[]{:S(2)}, u32[]{:S(2)}) collective-permute-start(bf16[4,2,9216]{2,1,0:T(2,128)(2,1)S(1)} %get-tuple-element.16.block_refs_0_), channel_id=1, source_target_pairs={{0,1},{1,0},{2,3},{3,2},{4,5},{5,4},{6,7},{7,6},{8,9},{9,8},{10,11... | collective-permute-start | bytes 442376 | tf_op jit(solution)/shard_map/ppermute | solution.py:234
  12.8 0.0 collective-permute-start.4
  12.8 1.2 %collective-permute-done.4.other_ref = f32[4,2,2,128]{3,2,1,0:T(2,128)S(1)} collective-permute-done((f32[4,2,2,128]{3,2,1,0:T(2,128)S(1)}, f32[4,2,2,128]{3,2,1,0:T(2,128)S(1)}, u32[]{:S(2)}, u32[]{:S(2)}) %collective-permute-start.4) | collective-permute-done | bytes 8224 | tf_op jit(solution)/shard_map/ppermute | solution.py:235
  14.0 0.6 %collective-permute-start.5 = (f32[4,2,2,128]{3,2,1,0:T(2,128)S(1)}, f32[4,2,2,128]{3,2,1,0:T(2,128)S(1)}, u32[]{:S(2)}, u32[]{:S(2)}) collective-permute-start(f32[4,2,2,128]{3,2,1,0:T(2,128)S(1)} %shard_map.66.stats_refs_0_), channel_id=1, source_target_pairs={{0,1},{1,0},{2,3},{3,2},{4,5},{5,4},{6,7},{7,6},{8,9},{9,8},{10,11... | collective-permute-start | bytes 24584 | tf_op jit(solution)/shard_map/ppermute | solution.py:247
  14.6 3.1 %collective-permute-done.5.stats_refs_1_ = f32[4,2,2,128]{3,2,1,0:T(2,128)S(1)} collective-permute-done((f32[4,2,2,128]{3,2,1,0:T(2,128)S(1)}, f32[4,2,2,128]{3,2,1,0:T(2,128)S(1)}, u32[]{:S(2)}, u32[]{:S(2)}) %collective-permute-start.5) | collective-permute-done | bytes 8224 | tf_op jit(solution)/shard_map/ppermute | solution.py:247
  17.7 0.0 collective-permute-done.3.block_refs_1_
  17.7 0.0 copy-done
  17.8 0.0 slice-start
  17.8 4.8 %shard_map.67 = f32[16,1,1600]{2,1,0:T(1,128)S(1)} custom-call(bf16[4,2,9216]{2,1,0:T(2,128)(2,1)S(1)} %get-tuple-element.16.block_refs_0_, bf16[4,2,9216]{2,1,0:T(2,128)(2,1)S(1)} %collective-permute-done.3.block_refs_1_, f32[4,2,2,128]{3,2,1,0:T(2,128)S(1)} %shard_map.66.stats_refs_0_, f32[4,2,2,128]{3,2,1,0:T(2,128)S(1)} %collective-permute-done.5.stats_refs_1_, ...), custom_call_target="tpu_custom_call" | custom-call | flops 471859200 | bytes 29491200 | tf_op jit(solution)/shard_map/pallas_call | solution.py:35
  22.6 10.2 %all_to_all.10.parts_ref = f32[16,1,1600]{2,1,0:T(1,128)S(1)} all-to-all(f32[16,1,1600]{2,1,0:T(1,128)S(1)} %shard_map.67), channel_id=1, replica_groups=mesh['ga'=2,'gx'=2,'yz'=8] {'yz','gx'}, dimensions={0} | all-to-all | bytes 204800 | tf_op jit(solution)/shard_map/all_to_all | solution.py:269
  32.8 0.0 copy-done.1
  32.8 0.0 slice-start.1
  32.8 0.0 slice-start.2
  32.8 0.0 slice-start.3
  32.8 0.0 slice-start.4
  32.8 0.0 slice-start.5
  32.8 0.0 slice-start.6
  32.8 0.5 %shard_map.68 = bf16[16,24,256]{2,1,0:T(8,128)(2,1)S(1)} custom-call(s32[8,128]{1,0:T(8,128)S(1)} %get-tuple-element.13.used_ref, f32[16,1,1600]{2,1,0:T(1,128)S(1)} %all_to_all.10.parts_ref, bf16[1,512,512]{2,1,0:T(8,128)(2,1)S(1)} %copy-done.1, ...), custom_call_target="tpu_custom_call" | custom-call | flops 25165824 | bytes 28311552 | tf_op jit(solution)/shard_map/pallas_call | solution.py:35
  33.3 12.1 %all_to_all.11.attended_ref = bf16[16,24,256]{2,1,0:T(8,128)(2,1)S(1)} all-to-all(bf16[16,24,256]{2,1,0:T(8,128)(2,1)S(1)} %shard_map.68), channel_id=1, replica_groups=mesh['ga'=2,'gx'=2,'yz'=8] {'yz','gx'}, dimensions={0} | all-to-all | bytes 393216 | tf_op jit(solution)/shard_map/all_to_all | solution.py:282
  45.5 0.0 slice-done
  45.5 0.0 slice-done.1
  45.5 0.0 slice-done.2
  45.5 0.0 slice-done.3
  45.5 0.0 slice-done.4
  45.5 0.0 slice-done.5
  45.5 0.0 slice-done.6
  45.5 3.8 %shard_map.69 = (f32[8,2304]{1,0:T(8,128)S(1)}, f32[8,2304]{1,0:T(8,128)S(1)}) custom-call(bf16[16,24,256]{2,1,0:T(8,128)(2,1)S(1)} %all_to_all.11.attended_ref, bf16[6144,2304]{1,0:T(8,128)(2,1)S(1)} %bitcast.4), custom_call_target="tpu_custom_call" | custom-call | flops 452984832 | bytes 28311552 | tf_op jit(solution)/shard_map/pallas_call | solution.py:35
  49.3 0.0 collective-permute-start.6
  49.3 1.3 %collective-permute-done.6 = f32[8,2304]{1,0:T(8,128)S(1)} collective-permute-done((f32[8,2304]{1,0:T(8,128)S(1)}, f32[8,2304]{1,0:T(8,128)S(1)}, u32[]{:S(2)}, u32[]{:S(2)}) %collective-permute-start.6) | collective-permute-done | bytes 73760 | tf_op jit(solution)/shard_map/ppermute | solution.py:297
  50.6 0.6 %add_convert_fusion = bf16[8,2304]{1,0:T(8,128)(2,1)} fusion(f32[8,2304]{1,0:T(8,128)S(1)} %get-tuple-element.19, f32[8,2304]{1,0:T(8,128)S(1)} %collective-permute-done.6), kind=kLoop, calls=%fused_computation | loop fusion | flops 36864 | bytes 184320 | tf_op jit(solution)/shard_map/convert_element_type | solution.py:298
  (2 shorter events, 0.0 us)
Async XLA Ops:
  0.0 17.8 %copy-start = (bf16[9216,1600]{0,1:T(8,128)(2,1)S(1)}, bf16[9216,1600]{0,1:T(8,128)(2,1)}, u32[]{:S(2)}) copy-start(bf16[9216,1600]{0,1:T(8,128)(2,1)} %param.8) | copy-start | bytes 88473600
  0.0 8.1 %collective-permute-start = (bf16[2,9216]{1,0:T(2,128)(2,1)}, bf16[2,9216]{1,0:T(2,128)(2,1)S(1)}, u32[]{:S(2)}, u32[]{:S(2)}) collective-permute-start(bf16[2,9216]{1,0:T(2,128)(2,1)} %tokens_hbm.1), channel_id=1, source_target_pairs={{0,2},{1,3},{2,0},{3,1},{4,6},{5,7},{6,4},{7,5},{8,10},{9,11},{10,... | collective-permute-start | bytes 110600 | tf_op jit(solution)/shard_map/ppermute | solution.py:220
  3.0 6.5 %collective-permute-start.2 = (bf16[2,9216]{1,0:T(2,128)(2,1)}, bf16[2,9216]{1,0:T(2,128)(2,1)S(1)}, u32[]{:S(2)}, u32[]{:S(2)}) collective-permute-start(bf16[2,9216]{1,0:T(2,128)(2,1)} %tokens_hbm.1), channel_id=1, source_target_pairs={{0,6},{1,7},{2,4},{3,5},{4,2},{5,3},{6,0},{7,1},{8,14},{9,15},{10,... | collective-permute-start | bytes 110600 | tf_op jit(solution)/shard_map/ppermute | solution.py:220
  5.5 5.5 %collective-permute-start.1 = (bf16[2,9216]{1,0:T(2,128)(2,1)}, bf16[2,9216]{1,0:T(2,128)(2,1)S(1)}, u32[]{:S(2)}, u32[]{:S(2)}) collective-permute-start(bf16[2,9216]{1,0:T(2,128)(2,1)} %tokens_hbm.1), channel_id=1, source_target_pairs={{0,4},{1,5},{2,6},{3,7},{4,0},{5,1},{6,2},{7,3},{8,12},{9,13},{10,... | collective-permute-start | bytes 110600 | tf_op jit(solution)/shard_map/ppermute | solution.py:220
  11.0 21.8 %copy-start.1 = (bf16[1,512,512]{2,1,0:T(8,128)(2,1)S(1)}, bf16[1,512,512]{2,1,0:T(8,128)(2,1)}, u32[]{:S(2)}) copy-start(bf16[1,512,512]{2,1,0:T(8,128)(2,1)} %cache_ref.1) | copy-start | bytes 1572868
  11.3 6.4 %collective-permute-start.3 = (bf16[4,2,9216]{2,1,0:T(2,128)(2,1)S(1)}, bf16[4,2,9216]{2,1,0:T(2,128)(2,1)S(1)}, u32[]{:S(2)}, u32[]{:S(2)}) collective-permute-start(bf16[4,2,9216]{2,1,0:T(2,128)(2,1)S(1)} %get-tuple-element.16.block_refs_0_), channel_id=1, source_target_pairs={{0,1},{1,0},{2,3},{3,2},{4,5},{5,4},{6,7},{7,6},{8,9},{9,8},{10,11... | collective-permute-start | bytes 442376 | tf_op jit(solution)/shard_map/ppermute | solution.py:234
  12.8 1.2 %collective-permute-start.4 = (f32[4,2,2,128]{3,2,1,0:T(2,128)S(1)}, f32[4,2,2,128]{3,2,1,0:T(2,128)S(1)}, u32[]{:S(2)}, u32[]{:S(2)}) collective-permute-start(f32[4,2,2,128]{3,2,1,0:T(2,128)S(1)} %get-tuple-element.17.sums_ref), channel_id=1, source_target_pairs={{0,8},{8,0},{1,9},{9,1},{2,10},{10,2},{3,11},{11,3},{4,12},{12,4},... | collective-permute-start | bytes 24584 | tf_op jit(solution)/shard_map/ppermute | solution.py:235
  14.0 3.7 %collective-permute-start.5 = (f32[4,2,2,128]{3,2,1,0:T(2,128)S(1)}, f32[4,2,2,128]{3,2,1,0:T(2,128)S(1)}, u32[]{:S(2)}, u32[]{:S(2)}) collective-permute-start(f32[4,2,2,128]{3,2,1,0:T(2,128)S(1)} %shard_map.66.stats_refs_0_), channel_id=1, source_target_pairs={{0,1},{1,0},{2,3},{3,2},{4,5},{5,4},{6,7},{7,6},{8,9},{9,8},{10,11... | collective-permute-start | bytes 24584 | tf_op jit(solution)/shard_map/ppermute | solution.py:247
  17.8 27.7 %slice-start = ((s8[28311552]{0:T(1024)(128)(4,1)}), s8[3145728]{0:T(1024)(128)(4,1)S(1)}, s32[]{:S(2)}) async-start(s8[28311552]{0:T(1024)(128)(4,1)} %bitcast.3), calls=%async_computation.2 | async-start | bytes 6291456
  32.8 12.7 %slice-start.1 = ((s8[28311552]{0:T(1024)(128)(4,1)}), s8[4194304]{0:T(1024)(128)(4,1)S(1)}, s32[]{:S(2)}) async-start(s8[28311552]{0:T(1024)(128)(4,1)} %bitcast.3), calls=%async_computation.3 | async-start | bytes 8388608
  32.8 12.7 %slice-start.2 = ((s8[28311552]{0:T(1024)(128)(4,1)}), s8[4194304]{0:T(1024)(128)(4,1)S(1)}, s32[]{:S(2)}) async-start(s8[28311552]{0:T(1024)(128)(4,1)} %bitcast.3), calls=%async_computation.4 | async-start | bytes 8388608
  32.8 12.7 %slice-start.3 = ((s8[28311552]{0:T(1024)(128)(4,1)}), s8[4194304]{0:T(1024)(128)(4,1)S(1)}, s32[]{:S(2)}) async-start(s8[28311552]{0:T(1024)(128)(4,1)} %bitcast.3), calls=%async_computation.5 | async-start | bytes 8388608
  32.8 12.7 %slice-start.4 = ((s8[28311552]{0:T(1024)(128)(4,1)}), s8[4194304]{0:T(1024)(128)(4,1)S(1)}, s32[]{:S(2)}) async-start(s8[28311552]{0:T(1024)(128)(4,1)} %bitcast.3), calls=%async_computation.6 | async-start | bytes 8388608
  32.8 12.7 %slice-start.5 = ((s8[28311552]{0:T(1024)(128)(4,1)}), s8[4194304]{0:T(1024)(128)(4,1)S(1)}, s32[]{:S(2)}) async-start(s8[28311552]{0:T(1024)(128)(4,1)} %bitcast.3), calls=%async_computation.7 | async-start | bytes 8388608
  32.8 12.7 %slice-start.6 = ((s8[28311552]{0:T(1024)(128)(4,1)}), s8[4194304]{0:T(1024)(128)(4,1)S(1)}, s32[]{:S(2)}) async-start(s8[28311552]{0:T(1024)(128)(4,1)} %bitcast.3), calls=%async_computation.8 | async-start | bytes 8388608
  49.3 1.3 %collective-permute-start.6 = (f32[8,2304]{1,0:T(8,128)S(1)}, f32[8,2304]{1,0:T(8,128)S(1)}, u32[]{:S(2)}, u32[]{:S(2)}) collective-permute-start(f32[8,2304]{1,0:T(8,128)S(1)} %get-tuple-element.20), channel_id=1, source_target_pairs={{0,8},{8,0},{1,9},{9,1},{2,10},{10,2},{3,11},{11,3},{4,12},{12,4},... | collective-permute-start | bytes 221192 | tf_op jit(solution)/shard_map/ppermute | solution.py:297

commit v6 on v5

--- a/solution.py
+++ b/solution.py
@@ -57,21 +57,22 @@
         copy.wait()
 
 
-def column_kernel(rows_refs, spare_hbm, column_ref, sums_ref):
-    lanes = sums_ref.shape[2:]
+def column_kernel(rows_refs, spare_hbm, column_ref, sums_ref, wide):
     for i, ref in enumerate(rows_refs):
-        column_ref[i] = ref[...]
-        rows = ref[...].astype(jnp.float32)
-        sums_ref[i, 0] = jnp.broadcast_to(jnp.sum(rows, axis=1, keepdims=True), lanes)
-        sums_ref[i, 1] = jnp.broadcast_to(jnp.sum(rows * rows, axis=1, keepdims=True), lanes)
+        per = ref.shape[0]
+        wide[i * per : (i + 1) * per, :] = ref[...].astype(jnp.float32)
+    rows = wide[...]
+    column_ref[...] = rows.astype(jnp.bfloat16)
+    lanes = sums_ref.shape[1:]
+    sums_ref[0] = jnp.broadcast_to(jnp.sum(rows, axis=1, keepdims=True), lanes)
+    sums_ref[1] = jnp.broadcast_to(jnp.sum(rows * rows, axis=1, keepdims=True), lanes)
 
 
 def stats_kernel(sums_ref, other_ref, stats_ref):
-    for i in range(sums_ref.shape[0]):
-        mean = (sums_ref[i, 0] + other_ref[i, 0]) / D
-        var = (sums_ref[i, 1] + other_ref[i, 1]) / D - mean * mean
-        stats_ref[i, 0] = mean
-        stats_ref[i, 1] = lax.rsqrt(var + 1e-06)
+    mean = (sums_ref[0] + other_ref[0]) / D
+    var = (sums_ref[1] + other_ref[1]) / D - mean * mean
+    stats_ref[0] = mean
+    stats_ref[1] = lax.rsqrt(var + 1e-06)
 
 
 def dot_last(left, right):
@@ -81,28 +82,32 @@
 
 
 def project_kernel(
-    order, block_refs, stats_refs, gain_ref, weight_ref, out_ref, wide, stats, rows, terms
+    per, order, block_refs, stats_refs, gain_ref, weight_ref, out_ref, rows, terms
 ):
     group = lax.axis_index("yz")
-    at, places = 0, []
-    for ref, stats_ref, origins in zip(block_refs, stats_refs, order):
-        per = ref.shape[1]
-        for i, origin in enumerate(origins):
-            wide[at : at + per, :] = ref[i].astype(jnp.float32)
-            stats[0, at : at + per, :] = stats_ref[i, 0]
-            stats[1, at : at + per, :] = stats_ref[i, 1]
-            places.extend(origin(group) * per + r for r in range(per))
-            at += per
-    mean, scale = stats[0][:, 0:1], stats[1][:, 0:1]
-    rows[...] = ((wide[...] - mean) * scale * gain_ref[...]).astype(jnp.bfloat16)
+    places = [origin(group) * per + r for group_of in order for origin in group_of for r in range(per)]
     batch, depth = rows.shape
     width = weight_ref.shape[0]
+
+    def normalise(k):
+        cut = slice(k, k + BLOCK)
+        parts = []
+        for ref, stats_ref in zip(block_refs, stats_refs):
+            mean, scale = stats_ref[0][:, 0:1], stats_ref[1][:, 0:1]
+            parts.append((ref[:, cut].astype(jnp.float32) - mean) * scale * gain_ref[:, cut])
+        rows[:, cut] = jnp.concatenate(parts, axis=0).astype(jnp.bfloat16)
+
+    if width < 2 * BLOCK:
+        for k in range(0, depth, BLOCK):
+            normalise(k)
     at = 0
     while width - at >= 2 * BLOCK:
         middle, end = at + BLOCK, at + 2 * BLOCK
         first = jnp.zeros((batch, BLOCK), jnp.float32)
         second = jnp.zeros((BLOCK, batch), jnp.float32)
         for k in range(0, depth, BLOCK):
+            if at == 0:
+                normalise(k)
             some = rows[:, k : k + BLOCK]
             second = second + dot_last(weight_ref[middle:end, k : k + BLOCK], some)
             first = first + dot_last(some, weight_ref[at:middle, k : k + BLOCK])
@@ -221,12 +226,12 @@
         column, sums = call(
             column_kernel,
             [
-                jax.ShapeDtypeStruct((len(steps), per, depth), bf16),
-                jax.ShapeDtypeStruct((len(steps), 2, per, 128), f32),
+                jax.ShapeDtypeStruct((batch // 2, depth), bf16),
+                jax.ShapeDtypeStruct((2, batch // 2, 128), f32),
             ],
             [[VMEM] * len(steps), ANY],
-            [],
-            bytes_of(((8, depth), 16)),
+            [pltpu.VMEM((batch // 2, depth), f32)],
+            bytes_of(((8, depth), 8), ((batch, depth), 4)),
             (4 * batch * depth, 4 * batch * depth),
             mates,
             spare,
@@ -250,12 +255,10 @@
             [lambda g, k=k: g ^ k ^ 1 for k in steps],
         ]
         parts = call(
-            functools.partial(project_kernel, order),
+            functools.partial(project_kernel, per, order),
             jax.ShapeDtypeStruct((members, 1, width), f32),
             [[VMEM] * len(blocks), [VMEM] * len(blocks), VMEM, VMEM],
             [
-                pltpu.VMEM((batch, depth), f32),
-                pltpu.VMEM((2, batch, 128), f32),
                 pltpu.VMEM((batch, depth), bf16),
                 pltpu.VMEM((batch, width), f32),
             ],

time: 51.4 us -> 51 us (level)
  no operation moved by 1% of the time
where the time goes in v6:
time: 51 us; the launch traced here: 50.8 us
  blocking collectives  22.3 us (44%)
  Pallas kernels  10.3 us (20%)
  waiting for transfers between devices  8.42 us (17%)
  starting transfers between devices  7.65 us (15%)
  between operations  1.52 us (3%)
  other arithmetic  0.63 us (1%)
    all_to_all x1, blocking collectives, on_device(): gathered = lax.all_to_all(attended, ('yz', 'gx'), 0, 0, tiled=True)  12.1 us
    pallas_call x6, Pallas kernels, call(): pl.pallas_call(kernel, out_shape=outs, in_specs=in_specs, out_specs=jax.t...  10.3 us
    all_to_all x1, blocking collectives, on_device(): moved = lax.all_to_all(parts, ('yz', 'gx'), 0, 0, tiled=True)  10.2 us
    ppermute x3, starting transfers between devices, on_device(): mates = [own] + [lax.ppermute(tokens, 'yz', pairs(k)) for k in steps[1:]]  5.62 us
    ppermute x1, waiting for transfers between devices, on_device(): scales = [stats, lax.ppermute(stats, 'yz', pairs(1))]  3.12 us
    ppermute x3, waiting for transfers between devices, on_device(): mates = [own] + [lax.ppermute(tokens, 'yz', pairs(k)) for k in steps[1:]]  2.86 us
    ppermute x1, starting transfers between devices, on_device(): beside = lax.ppermute(column, 'yz', pairs(1))  1.49 us
    ppermute x1, waiting for transfers between devices, on_device(): got = lax.ppermute(given, 'gx', swap)  1.27 us
  transfers between devices with their start and end apart: 7, of which 5 were waited for; matrix products, arithmetic and copies ran while one was open for 0% of the time, Pallas kernels for 2%

profile of v6, /device:TPU:0, one launch (start us, length us, event | category | flops | bytes accessed | tf_op | source)
XLA Modules:
  0.0 50.8 jit_solution(14580726115297540313)
XLA Ops:
  0.0 0.0 copy-start
  0.0 3.0 %collective-permute-start = (bf16[2,9216]{1,0:T(2,128)(2,1)}, bf16[2,9216]{1,0:T(2,128)(2,1)S(1)}, u32[]{:S(2)}, u32[]{:S(2)}) collective-permute-start(bf16[2,9216]{1,0:T(2,128)(2,1)} %tokens_hbm.1), channel_id=1, source_target_pairs={{0,2},{1,3},{2,0},{3,1},{4,6},{5,7},{6,4},{7,5},{8,10},{9,11},{10,... | collective-permute-start | bytes 110600 | tf_op jit(solution)/shard_map/ppermute | solution.py:225
  3.0 2.5 %collective-permute-start.2 = (bf16[2,9216]{1,0:T(2,128)(2,1)}, bf16[2,9216]{1,0:T(2,128)(2,1)S(1)}, u32[]{:S(2)}, u32[]{:S(2)}) collective-permute-start(bf16[2,9216]{1,0:T(2,128)(2,1)} %tokens_hbm.1), channel_id=1, source_target_pairs={{0,6},{1,7},{2,4},{3,5},{4,2},{5,3},{6,0},{7,1},{8,14},{9,15},{10,... | collective-permute-start | bytes 110600 | tf_op jit(solution)/shard_map/ppermute | solution.py:225
  5.5 0.1 collective-permute-start.1
  7.0 1.1 %shard_map.64 = (bf16[2,9216]{1,0:T(2,128)(2,1)S(1)}, f32[1,9216]{1,0:T(1,128)S(1)}, s32[8,128]{1,0:T(8,128)S(1)}, bf16[18000,1024]{1,0:T(8,128)(2,1)}) custom-call(s32[1]{0:T(128)S(6)} %copy.7.lengths_ref, bf16[2,9216]{1,0:T(2,128)(2,1)} %tokens_hbm.1, f32[1,9216]{1,0:T(1,128)} %bitcast.5), custom_call_target="tpu_custom_call" | custom-call | flops 18432 | bytes 36864 | tf_op jit(solution)/shard_map/pallas_call | solution.py:35
  8.1 0.0 collective-permute-done.rows_refs_1_
  8.1 1.4 %collective-permute-done.2.rows_refs_3_ = bf16[2,9216]{1,0:T(2,128)(2,1)S(1)} collective-permute-done((bf16[2,9216]{1,0:T(2,128)(2,1)}, bf16[2,9216]{1,0:T(2,128)(2,1)S(1)}, u32[]{:S(2)}, u32[]{:S(2)}) %collective-permute-start.2) | collective-permute-done | bytes 36896 | tf_op jit(solution)/shard_map/ppermute | solution.py:225
  9.5 1.5 %collective-permute-done.1.rows_refs_2_ = bf16[2,9216]{1,0:T(2,128)(2,1)S(1)} collective-permute-done((bf16[2,9216]{1,0:T(2,128)(2,1)}, bf16[2,9216]{1,0:T(2,128)(2,1)S(1)}, u32[]{:S(2)}, u32[]{:S(2)}) %collective-permute-start.1) | collective-permute-done | bytes 36896 | tf_op jit(solution)/shard_map/ppermute | solution.py:225
  11.0 0.0 copy-start.1
  11.0 0.2 shard_map.65
  11.2 1.5 %collective-permute-start.3 = (bf16[8,9216]{1,0:T(8,128)(2,1)S(1)}, bf16[8,9216]{1,0:T(8,128)(2,1)S(1)}, u32[]{:S(2)}, u32[]{:S(2)}) collective-permute-start(bf16[8,9216]{1,0:T(8,128)(2,1)S(1)} %get-tuple-element.16.block_refs_0_), channel_id=1, source_target_pairs={{0,1},{1,0},{2,3},{3,2},{4,5},{5,4},{6,7},{7,6},{8,9},{9,8},{10,11... | collective-permute-start | bytes 442376 | tf_op jit(solution)/shard_map/ppermute | solution.py:239
  12.7 0.0 collective-permute-start.4
  12.7 1.2 %collective-permute-done.4.other_ref = f32[2,8,128]{2,1,0:T(8,128)S(1)} collective-permute-done((f32[2,8,128]{2,1,0:T(8,128)S(1)}, f32[2,8,128]{2,1,0:T(8,128)S(1)}, u32[]{:S(2)}, u32[]{:S(2)}) %collective-permute-start.4) | collective-permute-done | bytes 8224 | tf_op jit(solution)/shard_map/ppermute | solution.py:240
  13.9 0.5 %collective-permute-start.5 = (f32[2,8,128]{2,1,0:T(8,128)S(1)}, f32[2,8,128]{2,1,0:T(8,128)S(1)}, u32[]{:S(2)}, u32[]{:S(2)}) collective-permute-start(f32[2,8,128]{2,1,0:T(8,128)S(1)} %shard_map.66.stats_refs_0_), channel_id=1, source_target_pairs={{0,1},{1,0},{2,3},{3,2},{4,5},{5,4},{6,7},{7,6},{8,9},{9,8},{10,11... | collective-permute-start | bytes 24584 | tf_op jit(solution)/shard_map/ppermute | solution.py:252
  14.4 3.1 %collective-permute-done.5.stats_refs_1_ = f32[2,8,128]{2,1,0:T(8,128)S(1)} collective-permute-done((f32[2,8,128]{2,1,0:T(8,128)S(1)}, f32[2,8,128]{2,1,0:T(8,128)S(1)}, u32[]{:S(2)}, u32[]{:S(2)}) %collective-permute-start.5) | collective-permute-done | bytes 8224 | tf_op jit(solution)/shard_map/ppermute | solution.py:252
  17.5 0.0 collective-permute-done.3.block_refs_1_
  17.5 0.0 copy-done
  17.5 0.0 slice-start
  17.6 4.6 %shard_map.67 = f32[16,1,1600]{2,1,0:T(1,128)S(1)} custom-call(bf16[8,9216]{1,0:T(8,128)(2,1)S(1)} %get-tuple-element.16.block_refs_0_, bf16[8,9216]{1,0:T(8,128)(2,1)S(1)} %collective-permute-done.3.block_refs_1_, f32[2,8,128]{2,1,0:T(8,128)S(1)} %shard_map.66.stats_refs_0_, f32[2,8,128]{2,1,0:T(8,128)S(1)} %collective-permute-done.5.stats_refs_1_, ...), custom_call_target="tpu_custom_call" | custom-call | flops 471859200 | bytes 29491200 | tf_op jit(solution)/shard_map/pallas_call | solution.py:35
  22.2 10.2 %all_to_all.10.parts_ref = f32[16,1,1600]{2,1,0:T(1,128)S(1)} all-to-all(f32[16,1,1600]{2,1,0:T(1,128)S(1)} %shard_map.67), channel_id=1, replica_groups=mesh['ga'=2,'gx'=2,'yz'=8] {'yz','gx'}, dimensions={0} | all-to-all | bytes 204800 | tf_op jit(solution)/shard_map/all_to_all | solution.py:272
  32.4 0.0 copy-done.1
  32.4 0.0 slice-start.1
  32.4 0.0 slice-start.2
  32.4 0.0 slice-start.3
  32.4 0.0 slice-start.4
  32.4 0.0 slice-start.5
  32.4 0.0 slice-start.6
  32.4 0.5 %shard_map.68 = bf16[16,24,256]{2,1,0:T(8,128)(2,1)S(1)} custom-call(s32[8,128]{1,0:T(8,128)S(1)} %get-tuple-element.13.used_ref, f32[16,1,1600]{2,1,0:T(1,128)S(1)} %all_to_all.10.parts_ref, bf16[1,512,512]{2,1,0:T(8,128)(2,1)S(1)} %copy-done.1, ...), custom_call_target="tpu_custom_call" | custom-call | flops 25165824 | bytes 28311552 | tf_op jit(solution)/shard_map/pallas_call | solution.py:35
  32.9 12.1 %all_to_all.11.attended_ref = bf16[16,24,256]{2,1,0:T(8,128)(2,1)S(1)} all-to-all(bf16[16,24,256]{2,1,0:T(8,128)(2,1)S(1)} %shard_map.68), channel_id=1, replica_groups=mesh['ga'=2,'gx'=2,'yz'=8] {'yz','gx'}, dimensions={0} | all-to-all | bytes 393216 | tf_op jit(solution)/shard_map/all_to_all | solution.py:285
  45.1 0.0 slice-done
  45.1 0.0 slice-done.1
  45.1 0.0 slice-done.2
  45.1 0.0 slice-done.3
  45.1 0.0 slice-done.4
  45.1 0.0 slice-done.5
  45.1 0.0 slice-done.6
  45.1 3.8 %shard_map.69 = (f32[8,2304]{1,0:T(8,128)S(1)}, f32[8,2304]{1,0:T(8,128)S(1)}) custom-call(bf16[16,24,256]{2,1,0:T(8,128)(2,1)S(1)} %all_to_all.11.attended_ref, bf16[6144,2304]{1,0:T(8,128)(2,1)S(1)} %bitcast.4), custom_call_target="tpu_custom_call" | custom-call | flops 452984832 | bytes 28311552 | tf_op jit(solution)/shard_map/pallas_call | solution.py:35
  48.9 0.0 collective-permute-start.6
  48.9 1.3 %collective-permute-done.6 = f32[8,2304]{1,0:T(8,128)S(1)} collective-permute-done((f32[8,2304]{1,0:T(8,128)S(1)}, f32[8,2304]{1,0:T(8,128)S(1)}, u32[]{:S(2)}, u32[]{:S(2)}) %collective-permute-start.6) | collective-permute-done | bytes 73760 | tf_op jit(solution)/shard_map/ppermute | solution.py:300
  50.2 0.6 %add_convert_fusion = bf16[8,2304]{1,0:T(8,128)(2,1)} fusion(f32[8,2304]{1,0:T(8,128)S(1)} %get-tuple-element.19, f32[8,2304]{1,0:T(8,128)S(1)} %collective-permute-done.6), kind=kLoop, calls=%fused_computation | loop fusion | flops 36864 | bytes 184320 | tf_op jit(solution)/shard_map/convert_element_type | solution.py:301
  (2 shorter events, 0.0 us)
Async XLA Ops:
  0.0 17.5 %copy-start = (bf16[9216,1600]{0,1:T(8,128)(2,1)S(1)}, bf16[9216,1600]{0,1:T(8,128)(2,1)}, u32[]{:S(2)}) copy-start(bf16[9216,1600]{0,1:T(8,128)(2,1)} %param.8) | copy-start | bytes 88473600
  0.0 8.1 %collective-permute-start = (bf16[2,9216]{1,0:T(2,128)(2,1)}, bf16[2,9216]{1,0:T(2,128)(2,1)S(1)}, u32[]{:S(2)}, u32[]{:S(2)}) collective-permute-start(bf16[2,9216]{1,0:T(2,128)(2,1)} %tokens_hbm.1), channel_id=1, source_target_pairs={{0,2},{1,3},{2,0},{3,1},{4,6},{5,7},{6,4},{7,5},{8,10},{9,11},{10,... | collective-permute-start | bytes 110600 | tf_op jit(solution)/shard_map/ppermute | solution.py:225
  3.0 6.5 %collective-permute-start.2 = (bf16[2,9216]{1,0:T(2,128)(2,1)}, bf16[2,9216]{1,0:T(2,128)(2,1)S(1)}, u32[]{:S(2)}, u32[]{:S(2)}) collective-permute-start(bf16[2,9216]{1,0:T(2,128)(2,1)} %tokens_hbm.1), channel_id=1, source_target_pairs={{0,6},{1,7},{2,4},{3,5},{4,2},{5,3},{6,0},{7,1},{8,14},{9,15},{10,... | collective-permute-start | bytes 110600 | tf_op jit(solution)/shard_map/ppermute | solution.py:225
  5.5 5.5 %collective-permute-start.1 = (bf16[2,9216]{1,0:T(2,128)(2,1)}, bf16[2,9216]{1,0:T(2,128)(2,1)S(1)}, u32[]{:S(2)}, u32[]{:S(2)}) collective-permute-start(bf16[2,9216]{1,0:T(2,128)(2,1)} %tokens_hbm.1), channel_id=1, source_target_pairs={{0,4},{1,5},{2,6},{3,7},{4,0},{5,1},{6,2},{7,3},{8,12},{9,13},{10,... | collective-permute-start | bytes 110600 | tf_op jit(solution)/shard_map/ppermute | solution.py:225
  11.0 21.4 %copy-start.1 = (bf16[1,512,512]{2,1,0:T(8,128)(2,1)S(1)}, bf16[1,512,512]{2,1,0:T(8,128)(2,1)}, u32[]{:S(2)}) copy-start(bf16[1,512,512]{2,1,0:T(8,128)(2,1)} %cache_ref.1) | copy-start | bytes 1572868
  11.2 6.3 %collective-permute-start.3 = (bf16[8,9216]{1,0:T(8,128)(2,1)S(1)}, bf16[8,9216]{1,0:T(8,128)(2,1)S(1)}, u32[]{:S(2)}, u32[]{:S(2)}) collective-permute-start(bf16[8,9216]{1,0:T(8,128)(2,1)S(1)} %get-tuple-element.16.block_refs_0_), channel_id=1, source_target_pairs={{0,1},{1,0},{2,3},{3,2},{4,5},{5,4},{6,7},{7,6},{8,9},{9,8},{10,11... | collective-permute-start | bytes 442376 | tf_op jit(solution)/shard_map/ppermute | solution.py:239
  12.7 1.2 %collective-permute-start.4 = (f32[2,8,128]{2,1,0:T(8,128)S(1)}, f32[2,8,128]{2,1,0:T(8,128)S(1)}, u32[]{:S(2)}, u32[]{:S(2)}) collective-permute-start(f32[2,8,128]{2,1,0:T(8,128)S(1)} %get-tuple-element.17.sums_ref), channel_id=1, source_target_pairs={{0,8},{8,0},{1,9},{9,1},{2,10},{10,2},{3,11},{11,3},{4,12},{12,4},... | collective-permute-start | bytes 24584 | tf_op jit(solution)/shard_map/ppermute | solution.py:240
  13.9 3.7 %collective-permute-start.5 = (f32[2,8,128]{2,1,0:T(8,128)S(1)}, f32[2,8,128]{2,1,0:T(8,128)S(1)}, u32[]{:S(2)}, u32[]{:S(2)}) collective-permute-start(f32[2,8,128]{2,1,0:T(8,128)S(1)} %shard_map.66.stats_refs_0_), channel_id=1, source_target_pairs={{0,1},{1,0},{2,3},{3,2},{4,5},{5,4},{6,7},{7,6},{8,9},{9,8},{10,11... | collective-permute-start | bytes 24584 | tf_op jit(solution)/shard_map/ppermute | solution.py:252
  17.5 27.5 %slice-start = ((s8[28311552]{0:T(1024)(128)(4,1)}), s8[3145728]{0:T(1024)(128)(4,1)S(1)}, s32[]{:S(2)}) async-start(s8[28311552]{0:T(1024)(128)(4,1)} %bitcast.3), calls=%async_computation.2 | async-start | bytes 6291456
  32.4 12.7 %slice-start.1 = ((s8[28311552]{0:T(1024)(128)(4,1)}), s8[4194304]{0:T(1024)(128)(4,1)S(1)}, s32[]{:S(2)}) async-start(s8[28311552]{0:T(1024)(128)(4,1)} %bitcast.3), calls=%async_computation.3 | async-start | bytes 8388608
  32.4 12.7 %slice-start.2 = ((s8[28311552]{0:T(1024)(128)(4,1)}), s8[4194304]{0:T(1024)(128)(4,1)S(1)}, s32[]{:S(2)}) async-start(s8[28311552]{0:T(1024)(128)(4,1)} %bitcast.3), calls=%async_computation.4 | async-start | bytes 8388608
  32.4 12.7 %slice-start.3 = ((s8[28311552]{0:T(1024)(128)(4,1)}), s8[4194304]{0:T(1024)(128)(4,1)S(1)}, s32[]{:S(2)}) async-start(s8[28311552]{0:T(1024)(128)(4,1)} %bitcast.3), calls=%async_computation.5 | async-start | bytes 8388608
  32.4 12.7 %slice-start.4 = ((s8[28311552]{0:T(1024)(128)(4,1)}), s8[4194304]{0:T(1024)(128)(4,1)S(1)}, s32[]{:S(2)}) async-start(s8[28311552]{0:T(1024)(128)(4,1)} %bitcast.3), calls=%async_computation.6 | async-start | bytes 8388608
  32.4 12.7 %slice-start.5 = ((s8[28311552]{0:T(1024)(128)(4,1)}), s8[4194304]{0:T(1024)(128)(4,1)S(1)}, s32[]{:S(2)}) async-start(s8[28311552]{0:T(1024)(128)(4,1)} %bitcast.3), calls=%async_computation.7 | async-start | bytes 8388608
  32.4 12.7 %slice-start.6 = ((s8[28311552]{0:T(1024)(128)(4,1)}), s8[4194304]{0:T(1024)(128)(4,1)S(1)}, s32[]{:S(2)}) async-start(s8[28311552]{0:T(1024)(128)(4,1)} %bitcast.3), calls=%async_computation.8 | async-start | bytes 8388608
  48.9 1.3 %collective-permute-start.6 = (f32[8,2304]{1,0:T(8,128)S(1)}, f32[8,2304]{1,0:T(8,128)S(1)}, u32[]{:S(2)}, u32[]{:S(2)}) collective-permute-start(f32[8,2304]{1,0:T(8,128)S(1)} %get-tuple-element.20), channel_id=1, source_target_pairs={{0,8},{8,0},{1,9},{9,1},{2,10},{10,2},{3,11},{11,3},{4,12},{12,4},... | collective-permute-start | bytes 221192 | tf_op jit(solution)/shard_map/ppermute | solution.py:300

commit v7 on v6

--- a/solution.py
+++ b/solution.py
@@ -81,11 +81,7 @@
     )
 
 
-def project_kernel(
-    per, order, block_refs, stats_refs, gain_ref, weight_ref, out_ref, rows, terms
-):
-    group = lax.axis_index("yz")
-    places = [origin(group) * per + r for group_of in order for origin in group_of for r in range(per)]
+def project_kernel(block_refs, stats_refs, gain_ref, weight_ref, terms, rows):
     batch, depth = rows.shape
     width = weight_ref.shape[0]
 
@@ -116,11 +112,16 @@
         at = end
     if at < width:
         terms[:, at:] = dot_last(rows[...], weight_ref[at:, :])
+
+
+def place_kernel(per, order, terms_ref, spare_refs, out_ref):
+    group = lax.axis_index("yz")
+    places = [origin(group) * per + r for group_of in order for origin in group_of for r in range(per)]
     for i, place in enumerate(places):
-        out_ref[place] = terms[i : i + 1, :]
-
-
-def attend_kernel(halves, used_ref, parts_ref, cache_ref, spare_refs, out_ref, heads):
+        out_ref[place] = terms_ref[i : i + 1, :]
+
+
+def attend_kernel(halves, used_ref, parts_ref, cache_ref, out_ref, heads):
     width = parts_ref.shape[2]
     pieces = []
     for i in range(parts_ref.shape[0] // halves):
@@ -254,13 +255,12 @@
             [lambda g, k=k: g ^ k for k in steps],
             [lambda g, k=k: g ^ k ^ 1 for k in steps],
         ]
-        parts = call(
-            functools.partial(project_kernel, per, order),
-            jax.ShapeDtypeStruct((members, 1, width), f32),
+        terms = call(
+            project_kernel,
+            jax.ShapeDtypeStruct((batch, width), f32),
             [[VMEM] * len(blocks), [VMEM] * len(blocks), VMEM, VMEM],
             [
                 pltpu.VMEM((batch, depth), bf16),
-                pltpu.VMEM((batch, width), f32),
             ],
             bytes_of(((batch, depth), 12), ((batch, width + 128), 16), ((BLOCK, BLOCK), 8)),
             (2 * batch * depth * width, depth * width * 2),
@@ -269,18 +269,27 @@
             scale,
             w_in,
         )
+        parts = call(
+            functools.partial(place_kernel, per, order),
+            jax.ShapeDtypeStruct((members, 1, width), f32),
+            [VMEM, [ANY] * 7],
+            [],
+            bytes_of(((batch, width + 128), 16)),
+            (batch * width, 8 * batch * width),
+            terms,
+            [spare] * 7,
+        )
         moved = lax.all_to_all(parts, ("yz", "gx"), 0, 0, tiled=True)
         attended = call(
             functools.partial(attend_kernel, halves),
             jax.ShapeDtypeStruct((members, HQ // halves, HD), bf16),
-            [VMEM, VMEM, VMEM, [ANY] * 7],
+            [VMEM, VMEM, VMEM],
             [pltpu.VMEM((HQ + 8, HD), f32)],
             bytes_of(((members, HQ // halves, HD), 4), ((512, 512), 4), ((members, 8, width + 128), 8)),
             (4 * HQ * 512 * HD, w_out.shape[0] * wide_out * 2),
             used,
             moved,
             kv_cache,
-            [spare] * 7,
         )
         gathered = lax.all_to_all(attended, ("yz", "gx"), 0, 0, tiled=True)
         size = batch // halves

time: 51 us -> 51 us (level)
    all_to_all x1, blocking collectives: 12.1 us -> 11.6 us  [on_device(): gathered = lax.all_to_all(attended, ('yz', 'gx'), 0, 0, tiled=True)]
    pallas_call x6 -> x7, Pallas kernels: 10.3 us -> 10.3 us  [call(): pl.pallas_call(kernel, out_shape=outs, in_specs=in_specs, out_specs=jax.t...]
where the time goes in v7:
time: 51 us; the launch traced here: 50.8 us
  blocking collectives  22.2 us (44%)
  Pallas kernels  10.3 us (20%)
  waiting for transfers between devices  8.42 us (17%)
  starting transfers between devices  7.65 us (15%)
  between operations  1.53 us (3%)
  other arithmetic  0.63 us (1%)
    all_to_all x1, blocking collectives, on_device(): gathered = lax.all_to_all(attended, ('yz', 'gx'), 0, 0, tiled=True)  11.6 us
    all_to_all x1, blocking collectives, on_device(): moved = lax.all_to_all(parts, ('yz', 'gx'), 0, 0, tiled=True)  10.7 us
    pallas_call x7, Pallas kernels, call(): pl.pallas_call(kernel, out_shape=outs, in_specs=in_specs, out_specs=jax.t...  10.3 us
    ppermute x3, starting transfers between devices, on_device(): mates = [own] + [lax.ppermute(tokens, 'yz', pairs(k)) for k in steps[1:]]  5.62 us
    ppermute x1, waiting for transfers between devices, on_device(): scales = [stats, lax.ppermute(stats, 'yz', pairs(1))]  3.12 us
    ppermute x3, waiting for transfers between devices, on_device(): mates = [own] + [lax.ppermute(tokens, 'yz', pairs(k)) for k in steps[1:]]  2.86 us
    ppermute x1, starting transfers between devices, on_device(): beside = lax.ppermute(column, 'yz', pairs(1))  1.49 us
    ppermute x1, waiting for transfers between devices, on_device(): got = lax.ppermute(given, 'gx', swap)  1.27 us
  transfers between devices with their start and end apart: 7, of which 5 were waited for; matrix products, arithmetic and copies ran while one was open for 0% of the time, Pallas kernels for 2%

profile of v7, /device:TPU:0, one launch (start us, length us, event | category | flops | bytes accessed | tf_op | source)
XLA Modules:
  0.0 50.8 jit_solution(2176763816470309452)
XLA Ops:
  0.0 0.0 copy-start
  0.0 3.0 %collective-permute-start = (bf16[2,9216]{1,0:T(2,128)(2,1)}, bf16[2,9216]{1,0:T(2,128)(2,1)S(1)}, u32[]{:S(2)}, u32[]{:S(2)}) collective-permute-start(bf16[2,9216]{1,0:T(2,128)(2,1)} %tokens_hbm.1), channel_id=1, source_target_pairs={{0,2},{1,3},{2,0},{3,1},{4,6},{5,7},{6,4},{7,5},{8,10},{9,11},{10,... | collective-permute-start | bytes 110600 | tf_op jit(solution)/shard_map/ppermute | solution.py:226
  3.0 2.5 %collective-permute-start.2 = (bf16[2,9216]{1,0:T(2,128)(2,1)}, bf16[2,9216]{1,0:T(2,128)(2,1)S(1)}, u32[]{:S(2)}, u32[]{:S(2)}) collective-permute-start(bf16[2,9216]{1,0:T(2,128)(2,1)} %tokens_hbm.1), channel_id=1, source_target_pairs={{0,6},{1,7},{2,4},{3,5},{4,2},{5,3},{6,0},{7,1},{8,14},{9,15},{10,... | collective-permute-start | bytes 110600 | tf_op jit(solution)/shard_map/ppermute | solution.py:226
  5.5 0.1 collective-permute-start.1
  7.0 1.1 %shard_map.64 = (bf16[2,9216]{1,0:T(2,128)(2,1)S(1)}, f32[1,9216]{1,0:T(1,128)S(1)}, s32[8,128]{1,0:T(8,128)S(1)}, bf16[18000,1024]{1,0:T(8,128)(2,1)}) custom-call(s32[1]{0:T(128)S(6)} %copy.7.lengths_ref, bf16[2,9216]{1,0:T(2,128)(2,1)} %tokens_hbm.1, f32[1,9216]{1,0:T(1,128)} %bitcast.5), custom_call_target="tpu_custom_call" | custom-call | flops 18432 | bytes 36864 | tf_op jit(solution)/shard_map/pallas_call | solution.py:35
  8.1 0.0 collective-permute-done.rows_refs_1_
  8.1 1.4 %collective-permute-done.2.rows_refs_3_ = bf16[2,9216]{1,0:T(2,128)(2,1)S(1)} collective-permute-done((bf16[2,9216]{1,0:T(2,128)(2,1)}, bf16[2,9216]{1,0:T(2,128)(2,1)S(1)}, u32[]{:S(2)}, u32[]{:S(2)}) %collective-permute-start.2) | collective-permute-done | bytes 36896 | tf_op jit(solution)/shard_map/ppermute | solution.py:226
  9.5 1.5 %collective-permute-done.1.rows_refs_2_ = bf16[2,9216]{1,0:T(2,128)(2,1)S(1)} collective-permute-done((bf16[2,9216]{1,0:T(2,128)(2,1)}, bf16[2,9216]{1,0:T(2,128)(2,1)S(1)}, u32[]{:S(2)}, u32[]{:S(2)}) %collective-permute-start.1) | collective-permute-done | bytes 36896 | tf_op jit(solution)/shard_map/ppermute | solution.py:226
  11.0 0.2 shard_map.65
  11.2 1.5 %collective-permute-start.3 = (bf16[8,9216]{1,0:T(8,128)(2,1)S(1)}, bf16[8,9216]{1,0:T(8,128)(2,1)S(1)}, u32[]{:S(2)}, u32[]{:S(2)}) collective-permute-start(bf16[8,9216]{1,0:T(8,128)(2,1)S(1)} %get-tuple-element.16.block_refs_0_), channel_id=1, source_target_pairs={{0,1},{1,0},{2,3},{3,2},{4,5},{5,4},{6,7},{7,6},{8,9},{9,8},{10,11... | collective-permute-start | bytes 442376 | tf_op jit(solution)/shard_map/ppermute | solution.py:240
  12.7 0.0 collective-permute-start.4
  12.7 1.2 %collective-permute-done.4.other_ref = f32[2,8,128]{2,1,0:T(8,128)S(1)} collective-permute-done((f32[2,8,128]{2,1,0:T(8,128)S(1)}, f32[2,8,128]{2,1,0:T(8,128)S(1)}, u32[]{:S(2)}, u32[]{:S(2)}) %collective-permute-start.4) | collective-permute-done | bytes 8224 | tf_op jit(solution)/shard_map/ppermute | solution.py:241
  13.9 0.5 %collective-permute-start.5 = (f32[2,8,128]{2,1,0:T(8,128)S(1)}, f32[2,8,128]{2,1,0:T(8,128)S(1)}, u32[]{:S(2)}, u32[]{:S(2)}) collective-permute-start(f32[2,8,128]{2,1,0:T(8,128)S(1)} %shard_map.66.stats_refs_0_), channel_id=1, source_target_pairs={{0,1},{1,0},{2,3},{3,2},{4,5},{5,4},{6,7},{7,6},{8,9},{9,8},{10,11... | collective-permute-start | bytes 24584 | tf_op jit(solution)/shard_map/ppermute | solution.py:253
  14.4 3.1 %collective-permute-done.5.stats_refs_1_ = f32[2,8,128]{2,1,0:T(8,128)S(1)} collective-permute-done((f32[2,8,128]{2,1,0:T(8,128)S(1)}, f32[2,8,128]{2,1,0:T(8,128)S(1)}, u32[]{:S(2)}, u32[]{:S(2)}) %collective-permute-start.5) | collective-permute-done | bytes 8224 | tf_op jit(solution)/shard_map/ppermute | solution.py:253
  17.5 0.0 collective-permute-done.3.block_refs_1_
  17.5 0.0 copy-done
  17.5 0.0 slice-start
  17.5 4.6 %shard_map.67.terms_ref = f32[16,1600]{1,0:T(8,128)S(1)} custom-call(bf16[8,9216]{1,0:T(8,128)(2,1)S(1)} %get-tuple-element.16.block_refs_0_, bf16[8,9216]{1,0:T(8,128)(2,1)S(1)} %collective-permute-done.3.block_refs_1_, f32[2,8,128]{2,1,0:T(8,128)S(1)} %shard_map.66.stats_refs_0_, f32[2,8,128]{2,1,0:T(8,128)S(1)} %collective-permute-done.5.stats_refs_1_, ...), custom_call_target="tpu_custom_call" | custom-call | flops 471859200 | bytes 29491200 | tf_op jit(solution)/shard_map/pallas_call | solution.py:35
  22.2 0.0 copy-start.1
  22.2 0.0 slice-start.1
  22.2 0.0 slice-start.2
  22.2 0.0 slice-start.3
  22.2 0.0 slice-start.4
  22.2 0.0 slice-start.5
  22.2 0.0 slice-start.6
  22.3 10.7 %all_to_all.10.parts_ref = f32[16,1,1600]{2,1,0:T(1,128)S(1)} all-to-all(f32[16,1,1600]{2,1,0:T(1,128)S(1)} %shard_map.68), channel_id=1, replica_groups=mesh['ga'=2,'gx'=2,'yz'=8] {'yz','gx'}, dimensions={0} | all-to-all | bytes 204800 | tf_op jit(solution)/shard_map/all_to_all | solution.py:282
  32.9 0.0 copy-done.1
  32.9 0.5 %shard_map.69 = bf16[16,24,256]{2,1,0:T(8,128)(2,1)S(1)} custom-call(s32[8,128]{1,0:T(8,128)S(1)} %get-tuple-element.13.used_ref, f32[16,1,1600]{2,1,0:T(1,128)S(1)} %all_to_all.10.parts_ref, bf16[1,512,512]{2,1,0:T(8,128)(2,1)S(1)} %copy-done.1), custom_call_target="tpu_custom_call" | custom-call | flops 25165824 | bytes 28311552 | tf_op jit(solution)/shard_map/pallas_call | solution.py:35
  33.4 11.6 %all_to_all.11.attended_ref = bf16[16,24,256]{2,1,0:T(8,128)(2,1)S(1)} all-to-all(bf16[16,24,256]{2,1,0:T(8,128)(2,1)S(1)} %shard_map.69), channel_id=1, replica_groups=mesh['ga'=2,'gx'=2,'yz'=8] {'yz','gx'}, dimensions={0} | all-to-all | bytes 393216 | tf_op jit(solution)/shard_map/all_to_all | solution.py:294
  45.0 0.0 slice-done
  45.0 0.0 slice-done.1
  45.0 0.0 slice-done.2
  45.0 0.0 slice-done.3
  45.1 0.0 slice-done.4
  45.1 0.0 slice-done.5
  45.1 0.0 slice-done.6
  45.1 3.8 %shard_map.70 = (f32[8,2304]{1,0:T(8,128)S(1)}, f32[8,2304]{1,0:T(8,128)S(1)}) custom-call(bf16[16,24,256]{2,1,0:T(8,128)(2,1)S(1)} %all_to_all.11.attended_ref, bf16[6144,2304]{1,0:T(8,128)(2,1)S(1)} %bitcast.4), custom_call_target="tpu_custom_call" | custom-call | flops 452984832 | bytes 28311552 | tf_op jit(solution)/shard_map/pallas_call | solution.py:35
  48.9 0.0 collective-permute-start.6
  48.9 1.3 %collective-permute-done.6 = f32[8,2304]{1,0:T(8,128)S(1)} collective-permute-done((f32[8,2304]{1,0:T(8,128)S(1)}, f32[8,2304]{1,0:T(8,128)S(1)}, u32[]{:S(2)}, u32[]{:S(2)}) %collective-permute-start.6) | collective-permute-done | bytes 73760 | tf_op jit(solution)/shard_map/ppermute | solution.py:309
  50.2 0.6 %add_convert_fusion = bf16[8,2304]{1,0:T(8,128)(2,1)} fusion(f32[8,2304]{1,0:T(8,128)S(1)} %get-tuple-element.19, f32[8,2304]{1,0:T(8,128)S(1)} %collective-permute-done.6), kind=kLoop, calls=%fused_computation | loop fusion | flops 36864 | bytes 184320 | tf_op jit(solution)/shard_map/convert_element_type | solution.py:310
  (3 shorter events, 0.0 us)
Async XLA Ops:
  0.0 17.5 %copy-start = (bf16[9216,1600]{0,1:T(8,128)(2,1)S(1)}, bf16[9216,1600]{0,1:T(8,128)(2,1)}, u32[]{:S(2)}) copy-start(bf16[9216,1600]{0,1:T(8,128)(2,1)} %param.8) | copy-start | bytes 88473600
  0.0 8.1 %collective-permute-start = (bf16[2,9216]{1,0:T(2,128)(2,1)}, bf16[2,9216]{1,0:T(2,128)(2,1)S(1)}, u32[]{:S(2)}, u32[]{:S(2)}) collective-permute-start(bf16[2,9216]{1,0:T(2,128)(2,1)} %tokens_hbm.1), channel_id=1, source_target_pairs={{0,2},{1,3},{2,0},{3,1},{4,6},{5,7},{6,4},{7,5},{8,10},{9,11},{10,... | collective-permute-start | bytes 110600 | tf_op jit(solution)/shard_map/ppermute | solution.py:226
  3.0 6.5 %collective-permute-start.2 = (bf16[2,9216]{1,0:T(2,128)(2,1)}, bf16[2,9216]{1,0:T(2,128)(2,1)S(1)}, u32[]{:S(2)}, u32[]{:S(2)}) collective-permute-start(bf16[2,9216]{1,0:T(2,128)(2,1)} %tokens_hbm.1), channel_id=1, source_target_pairs={{0,6},{1,7},{2,4},{3,5},{4,2},{5,3},{6,0},{7,1},{8,14},{9,15},{10,... | collective-permute-start | bytes 110600 | tf_op jit(solution)/shard_map/ppermute | solution.py:226
  5.5 5.5 %collective-permute-start.1 = (bf16[2,9216]{1,0:T(2,128)(2,1)}, bf16[2,9216]{1,0:T(2,128)(2,1)S(1)}, u32[]{:S(2)}, u32[]{:S(2)}) collective-permute-start(bf16[2,9216]{1,0:T(2,128)(2,1)} %tokens_hbm.1), channel_id=1, source_target_pairs={{0,4},{1,5},{2,6},{3,7},{4,0},{5,1},{6,2},{7,3},{8,12},{9,13},{10,... | collective-permute-start | bytes 110600 | tf_op jit(solution)/shard_map/ppermute | solution.py:226
  11.2 6.3 %collective-permute-start.3 = (bf16[8,9216]{1,0:T(8,128)(2,1)S(1)}, bf16[8,9216]{1,0:T(8,128)(2,1)S(1)}, u32[]{:S(2)}, u32[]{:S(2)}) collective-permute-start(bf16[8,9216]{1,0:T(8,128)(2,1)S(1)} %get-tuple-element.16.block_refs_0_), channel_id=1, source_target_pairs={{0,1},{1,0},{2,3},{3,2},{4,5},{5,4},{6,7},{7,6},{8,9},{9,8},{10,11... | collective-permute-start | bytes 442376 | tf_op jit(solution)/shard_map/ppermute | solution.py:240
  12.7 1.2 %collective-permute-start.4 = (f32[2,8,128]{2,1,0:T(8,128)S(1)}, f32[2,8,128]{2,1,0:T(8,128)S(1)}, u32[]{:S(2)}, u32[]{:S(2)}) collective-permute-start(f32[2,8,128]{2,1,0:T(8,128)S(1)} %get-tuple-element.17.sums_ref), channel_id=1, source_target_pairs={{0,8},{8,0},{1,9},{9,1},{2,10},{10,2},{3,11},{11,3},{4,12},{12,4},... | collective-permute-start | bytes 24584 | tf_op jit(solution)/shard_map/ppermute | solution.py:241
  13.9 3.7 %collective-permute-start.5 = (f32[2,8,128]{2,1,0:T(8,128)S(1)}, f32[2,8,128]{2,1,0:T(8,128)S(1)}, u32[]{:S(2)}, u32[]{:S(2)}) collective-permute-start(f32[2,8,128]{2,1,0:T(8,128)S(1)} %shard_map.66.stats_refs_0_), channel_id=1, source_target_pairs={{0,1},{1,0},{2,3},{3,2},{4,5},{5,4},{6,7},{7,6},{8,9},{9,8},{10,11... | collective-permute-start | bytes 24584 | tf_op jit(solution)/shard_map/ppermute | solution.py:253
  17.5 27.5 %slice-start = ((s8[28311552]{0:T(1024)(128)(4,1)}), s8[3145728]{0:T(1024)(128)(4,1)S(1)}, s32[]{:S(2)}) async-start(s8[28311552]{0:T(1024)(128)(4,1)} %bitcast.3), calls=%async_computation.2 | async-start | bytes 6291456
  22.2 10.7 %copy-start.1 = (bf16[1,512,512]{2,1,0:T(8,128)(2,1)S(1)}, bf16[1,512,512]{2,1,0:T(8,128)(2,1)}, u32[]{:S(2)}) copy-start(bf16[1,512,512]{2,1,0:T(8,128)(2,1)} %cache_ref.1) | copy-start | bytes 1572868
  22.2 22.9 %slice-start.1 = ((s8[28311552]{0:T(1024)(128)(4,1)}), s8[4194304]{0:T(1024)(128)(4,1)S(1)}, s32[]{:S(2)}) async-start(s8[28311552]{0:T(1024)(128)(4,1)} %bitcast.3), calls=%async_computation.3 | async-start | bytes 8388608
  22.2 22.9 %slice-start.2 = ((s8[28311552]{0:T(1024)(128)(4,1)}), s8[4194304]{0:T(1024)(128)(4,1)S(1)}, s32[]{:S(2)}) async-start(s8[28311552]{0:T(1024)(128)(4,1)} %bitcast.3), calls=%async_computation.4 | async-start | bytes 8388608
  22.2 22.9 %slice-start.3 = ((s8[28311552]{0:T(1024)(128)(4,1)}), s8[4194304]{0:T(1024)(128)(4,1)S(1)}, s32[]{:S(2)}) async-start(s8[28311552]{0:T(1024)(128)(4,1)} %bitcast.3), calls=%async_computation.5 | async-start | bytes 8388608
  22.2 22.9 %slice-start.4 = ((s8[28311552]{0:T(1024)(128)(4,1)}), s8[4194304]{0:T(1024)(128)(4,1)S(1)}, s32[]{:S(2)}) async-start(s8[28311552]{0:T(1024)(128)(4,1)} %bitcast.3), calls=%async_computation.6 | async-start | bytes 8388608
  22.2 22.9 %slice-start.5 = ((s8[28311552]{0:T(1024)(128)(4,1)}), s8[4194304]{0:T(1024)(128)(4,1)S(1)}, s32[]{:S(2)}) async-start(s8[28311552]{0:T(1024)(128)(4,1)} %bitcast.3), calls=%async_computation.7 | async-start | bytes 8388608
  22.2 22.9 %slice-start.6 = ((s8[28311552]{0:T(1024)(128)(4,1)}), s8[4194304]{0:T(1024)(128)(4,1)S(1)}, s32[]{:S(2)}) async-start(s8[28311552]{0:T(1024)(128)(4,1)} %bitcast.3), calls=%async_computation.8 | async-start | bytes 8388608
  48.9 1.3 %collective-permute-start.6 = (f32[8,2304]{1,0:T(8,128)S(1)}, f32[8,2304]{1,0:T(8,128)S(1)}, u32[]{:S(2)}, u32[]{:S(2)}) collective-permute-start(f32[8,2304]{1,0:T(8,128)S(1)} %get-tuple-element.20), channel_id=1, source_target_pairs={{0,8},{8,0},{1,9},{9,1},{2,10},{10,2},{3,11},{11,3},{4,12},{12,4},... | collective-permute-start | bytes 221192 | tf_op jit(solution)/shard_map/ppermute | solution.py:309
